TPU v7x, 32 devices: a whole 2x2x4 slice. The times are simulated.
32 devices in a mesh: docs: 8 (over y, x, core), rep: 4 (over z).
Axes of the slice: x: 2, y: 2, z: 4, core: 2. Of those that a mesh axis runs over, the one named last changes fastest.
Arguments:
- embeds: bfloat16 [8192, 1024], P(('docs', 'rep'))
- cluster: int32 [8192], P(('docs', 'rep')), may hold values from 0 to 15, as said below
Outputs:
- top_sim: float32 [8192], P(('docs', 'rep'))
- dup_mass: float32 [8192], P(('docs', 'rep'))
Inputs may be any that keep to these rules, and one draw needn't show every extreme that they name: Cluster ids never fall along the documents and every id is used; each cluster has at most 3074 documents, and some cluster has exactly that many and meets five consecutive blocks of 1024 documents; no cluster meets more than five.
All inputs are finite; a program needn't handle non-finite values.
Results may differ from a plain program's by a relative error of at most 0.00057.
Values may be sent and summed in bfloat16 or wider, within the bound.
A program may use at most 64 MiB of HBM per device.

v0:
```python
import jax
import jax.numpy as jnp
from jax import lax
from jax.sharding import PartitionSpec as P

dup_scale = 8.0


def shifted(shard, axis, by):
    peers = lax.axis_size(axis)
    pairs = [(i, i + by) for i in range(peers) if 0 <= i + by < peers]
    return lax.ppermute(shard, axis, pairs)


def per_device(embeds, cluster):
    x = embeds.astype(jnp.float32)
    unit = (
        x * lax.rsqrt(jnp.mean(x * x, axis=1, keepdims=True) + 1e-06) * x.shape[1] ** (-0.5)
    ).astype(jnp.bfloat16)
    quarter = unit.shape[0]
    parts = lax.axis_size("rep")
    count = lax.axis_size("docs")
    block = quarter * parts
    mine = lax.axis_index("docs")
    part = lax.axis_index("rep")
    own, own_ids = (
        lax.all_gather(unit, "rep", axis=0, tiled=True),
        lax.all_gather(cluster, "rep", axis=0, tiled=True),
    )
    own_pos = mine * block + jnp.arange(block, dtype=jnp.int32)
    offsets = part * quarter + jnp.arange(quarter, dtype=jnp.int32)

    def tile(recv, recv_ids, recv_pos, valid):
        scores = lax.dot_general(
            own, recv, (((1,), (1,)), ((), ())), preferred_element_type=jnp.float32
        )
        mask = (
            (own_ids[:, None] == recv_ids[None, :])
            & (own_pos[:, None] != recv_pos[None, :])
            & valid
        )
        top = jnp.where(mask, scores, -1.0)
        mass = jnp.where(mask, jnp.exp(dup_scale * (scores - 1.0)), 0.0)
        return (
            jnp.max(top, axis=1),
            jnp.sum(mass, axis=1),
            jnp.max(top, axis=0),
            jnp.sum(mass, axis=0),
        )

    row_top, row_mass, unused_top, unused_mass = tile(unit, cluster, mine * block + offsets, True)
    mine_top = jnp.full((quarter,), -1.0, jnp.float32)
    for step in range(1, 5):
        for sign in (1, -1):
            recv, recv_ids = shifted((unit, cluster), "docs", sign * step)
            source = mine - sign * step
            valid = (source >= 0) & (source < count)
            part_top, part_mass, col_top, col_mass = tile(
                recv, recv_ids, source * block + offsets, valid
            )
            row_top = jnp.maximum(row_top, part_top)
            row_mass = row_mass + part_mass
    got_top, got_mass = (
        lax.all_to_all(
            row_top.reshape(parts, quarter), "rep", split_axis=0, concat_axis=0, tiled=True
        ),
        lax.all_to_all(
            row_mass.reshape(parts, quarter), "rep", split_axis=0, concat_axis=0, tiled=True
        ),
    )
    top_sim = jnp.maximum(mine_top, jnp.max(got_top, axis=0))
    dup_mass = jnp.sum(got_mass, axis=0)
    return (top_sim, dup_mass)


def solution(mesh):
    placed = (P(("docs", "rep"), None), P(("docs", "rep")))
    return jax.shard_map(
        per_device,
        mesh=mesh,
        in_specs=placed,
        out_specs=(P(("docs", "rep")), P(("docs", "rep"))),
        check_vma=False,
    )
```

profile of v0, /device:TPU:0, one launch (start us, length us, event | category | flops | bytes accessed | tf_op | source)
XLA Modules:
  0.0 139.1 jit_solution(6172180400321003495)
XLA Ops:
  7.2 1.2 fusion
  8.5 2.0 %fusion.2 = bf16[256,1024]{1,0:T(8,128)(2,1)} fusion(bf16[256,1024]{1,0:T(8,128)(2,1)} %param.2, f32[256]{0:T(256)S(1)} %add_rsqrt_fusion), kind=kLoop, calls=%fused_computation.4 | loop fusion | flops 1048576 | bytes 1049600 | tf_op jit(solution)/shard_map/convert_element_type | solution.py:19
  10.5 1.3 collective-permute-start.14
  11.8 2.4 %collective-permute-start = (s32[256]{0:T(256)S(1)}, s32[256]{0:T(256)S(1)}, u32[]{:S(2)}, u32[]{:S(2)}) collective-permute-start(s32[256]{0:T(256)S(1)} %copy-done.2), channel_id=1, source_target_pairs={{0,4},{4,8},{8,12},{12,16},{16,20},{20,24},{24,28},{1,5},{5,9},{9,... | collective-permute-start | bytes 3080 | tf_op jit(solution)/shard_map/ppermute | solution.py:12
  14.2 1.3 collective-permute-start.3
  15.5 1.3 collective-permute-start.2
  16.8 7.4 %collective-permute-start.5 = (bf16[256,1024]{1,0:T(8,128)(2,1)}, bf16[256,1024]{1,0:T(8,128)(2,1)S(1)}, u32[]{:S(2)}, u32[]{:S(2)}) collective-permute-start(bf16[256,1024]{1,0:T(8,128)(2,1)} %fusion.2), channel_id=1, source_target_pairs={{0,8},{4,12},{8,16},{12,20},{16,24},{20,28},{1,9},{5,13},{9,17},{1... | collective-permute-start | bytes 1572872 | tf_op jit(solution)/shard_map/ppermute | solution.py:12
  24.3 11.3 %all-gather = s32[4,1,256]{2,1,0:T(1,128)S(1)} all-gather(s32[1,1,256]{2,1,0:T(1,128)S(1)} %bitcast.25), channel_id=1, replica_groups=mesh['docs'=8,'rep'=4] {'rep'}, dimensions={0}, use_global_device_ids=true | all-gather | bytes 5120 | tf_op jit(solution)/shard_map/all_gather | solution.py:28
  35.6 23.7 %all-gather.3.cloned.1.call-done = bf16[1024,1024]{1,0:T(8,128)(2,1)} async-done(((bf16[256,1024]{1,0:T(8,128)(2,1)}), bf16[1024,1024]{1,0:T(8,128)(2,1)}) %all-gather.3.cloned.1.call-update) | async-done | bytes 2097168 | tf_op jit(solution)/shard_map/all_gather | solution.py:27
  59.4 2.6 %fusion.12 = f32[1024,256]{0,1:T(8,128)S(1)} fusion(bf16[1024,1024]{1,0:T(8,128)(2,1)} %all-gather.3.cloned.1.call-done, bf16[256,1024]{1,0:T(8,128)(2,1)} %fusion.2), kind=kOutput, calls=%fused_computation.47 | convolution fusion | flops 536870912 | bytes 3670016 | tf_op jit(solution)/shard_map/dot_general | solution.py:34
  61.9 1.8 %collective-permute-start.1 = (bf16[256,1024]{1,0:T(8,128)(2,1)S(1)}, bf16[256,1024]{1,0:T(8,128)(2,1)S(1)}, u32[]{:S(2)}, u32[]{:S(2)}) collective-permute-start(bf16[256,1024]{1,0:T(8,128)(2,1)S(1)} %copy-done.1), channel_id=1, source_target_pairs={{0,4},{4,8},{8,12},{12,16},{16,20},{20,24},{24,28},{1,5},{5,9},{9,... | collective-permute-start | bytes 1572872 | tf_op jit(solution)/shard_map/ppermute | solution.py:12
  63.7 0.8 fusion.13
  64.5 3.5 %collective-permute-start.4 = (s32[256]{0:T(256)S(1)}, s32[256]{0:T(256)S(1)}, u32[]{:S(2)}, u32[]{:S(2)}) collective-permute-start(s32[256]{0:T(256)S(1)} %copy-done.2), channel_id=1, source_target_pairs={{0,8},{4,12},{8,16},{12,20},{16,24},{20,28},{1,9},{5,13},{9,17},{1... | collective-permute-start | bytes 3080 | tf_op jit(solution)/shard_map/ppermute | solution.py:12
  68.1 0.8 fusion.14
  68.9 1.3 collective-permute-start.15
  70.2 1.3 collective-permute-start.6
  71.5 5.2 %collective-permute-start.9 = (bf16[256,1024]{1,0:T(8,128)(2,1)S(1)}, bf16[256,1024]{1,0:T(8,128)(2,1)S(1)}, u32[]{:S(2)}, u32[]{:S(2)}) collective-permute-start(bf16[256,1024]{1,0:T(8,128)(2,1)S(1)} %copy-done.1), channel_id=1, source_target_pairs={{0,12},{4,16},{8,20},{12,24},{16,28},{1,13},{5,17},{9,21},{13,25},... | collective-permute-start | bytes 1572872 | tf_op jit(solution)/shard_map/ppermute | solution.py:12
  76.7 3.7 %collective-permute-start.8 = (s32[256]{0:T(256)S(1)}, s32[256]{0:T(256)S(1)}, u32[]{:S(2)}, u32[]{:S(2)}) collective-permute-start(s32[256]{0:T(256)S(1)} %copy-done.2), channel_id=1, source_target_pairs={{0,12},{4,16},{8,20},{12,24},{16,28},{1,13},{5,17},{9,21},{13,25},... | collective-permute-start | bytes 3080 | tf_op jit(solution)/shard_map/ppermute | solution.py:12
  80.4 3.2 %select_reduce_fusion.7 = (f32[1024]{0:T(1024)S(1)}, f32[1024]{0:T(1024)S(1)}, f32[1024]{0:T(1024)S(1)}, f32[1024]{0:T(1024)S(1)}, f32[1024]{0:T(1024)S(1)}, /*i...) fusion(s32[1024]{0:T(1024)S(1)} %iota_add_fusion, s32[1024]{0:T(1024)S(1)} %bitcast.22, ...), kind=kOutput, calls=%fused_computation.12 | convolution fusion | flops 547086336 | bytes 5816323 | tf_op jit(solution)/shard_map/dot_general | solution.py:34
  83.6 1.3 collective-permute-start.11
  85.3 1.3 collective-permute-start.10
  86.6 1.1 select_reduce_fusion
  87.6 5.5 %collective-permute-start.13 = (bf16[256,1024]{1,0:T(8,128)(2,1)S(1)}, bf16[256,1024]{1,0:T(8,128)(2,1)S(1)}, u32[]{:S(2)}, u32[]{:S(2)}) collective-permute-start(bf16[256,1024]{1,0:T(8,128)(2,1)S(1)} %copy-done.1), channel_id=1, source_target_pairs={{0,16},{4,20},{8,24},{12,28},{1,17},{5,21},{9,25},{13,29},{2,18},{... | collective-permute-start | bytes 1572872 | tf_op jit(solution)/shard_map/ppermute | solution.py:12
  94.1 1.3 collective-permute-start.7
  96.1 8.4 %collective-permute-done.13 = bf16[256,1024]{1,0:T(8,128)(2,1)S(1)} collective-permute-done((bf16[256,1024]{1,0:T(8,128)(2,1)S(1)}, bf16[256,1024]{1,0:T(8,128)(2,1)S(1)}, u32[]{:S(2)}, u32[]{:S(2)}) %collective-permute-start.13) | collective-permute-done | bytes 524320 | tf_op jit(solution)/shard_map/ppermute | solution.py:12
  104.6 4.4 %collective-permute-start.12 = (s32[256]{0:T(256)S(1)}, s32[256]{0:T(256)S(1)}, u32[]{:S(2)}, u32[]{:S(2)}) collective-permute-start(s32[256]{0:T(256)S(1)} %copy-done.2), channel_id=1, source_target_pairs={{0,16},{4,20},{8,24},{12,28},{1,17},{5,21},{9,25},{13,29},{2,18},{... | collective-permute-start | bytes 3080 | tf_op jit(solution)/shard_map/ppermute | solution.py:12
  108.9 0.8 fusion.17
  110.2 3.3 %select_reduce_fusion.4 = (f32[1024]{0:T(1024)S(1)}, f32[1024]{0:T(1024)S(1)}, f32[1024]{0:T(1024)S(1)}, f32[1024]{0:T(1024)S(1)}, f32[1024]{0:T(1024)S(1)}, /*i...) fusion(s32[1024]{0:T(1024)S(1)} %iota_add_fusion, s32[1024]{0:T(1024)S(1)} %bitcast.24, ...), kind=kOutput, calls=%fused_computation.9 | convolution fusion | flops 547348480 | bytes 5816324 | tf_op jit(solution)/shard_map/dot_general | solution.py:34
  114.1 3.2 %all-to-all-start = ((f32[4,1,256]{2,1,0:T(1,128)}), f32[4,1,256]{2,1,0:T(1,128)S(1)}, u32[]{:S(2)}, u32[]{:S(2)}) async-start(f32[4,1,256]{2,1,0:T(1,128)} %bitcast.2), calls=%async_computation | async-start | bytes 8192 | tf_op jit(solution)/shard_map/all_to_all | solution.py:64
  118.0 5.0 %all-to-all-done = f32[4,1,256]{2,1,0:T(1,128)S(1)} async-done(((f32[4,1,256]{2,1,0:T(1,128)}), f32[4,1,256]{2,1,0:T(1,128)S(1)}, u32[]{:S(2)}, u32[]{:S(2)}) %all-to-all-start) | async-done | bytes 4128 | tf_op jit(solution)/shard_map/all_to_all | solution.py:64
  122.9 3.2 %all-to-all-start.1 = ((f32[4,1,256]{2,1,0:T(1,128)}), f32[4,1,256]{2,1,0:T(1,128)S(1)}, u32[]{:S(2)}, u32[]{:S(2)}) async-start(f32[4,1,256]{2,1,0:T(1,128)} %bitcast.3), calls=%async_computation.1 | async-start | bytes 8192 | tf_op jit(solution)/shard_map/all_to_all | solution.py:67
  126.7 4.9 %all-to-all-done.1 = f32[4,1,256]{2,1,0:T(1,128)S(1)} async-done(((f32[4,1,256]{2,1,0:T(1,128)}), f32[4,1,256]{2,1,0:T(1,128)S(1)}, u32[]{:S(2)}, u32[]{:S(2)}) %all-to-all-start.1) | async-done | bytes 4128 | tf_op jit(solution)/shard_map/all_to_all | solution.py:67
  (37 shorter events, 5.0 us)
Async XLA Ops:
  7.2 3.4 %copy-start.2 = (s32[256]{0:T(256)S(1)}, s32[256]{0:T(256)}, u32[]{:S(2)}) copy-start(s32[256]{0:T(256)} %param.3) | copy-start | bytes 3076
  7.2 52.2 %all-gather.3.cloned.1.call-start = ((), (), s32[]{:S(2)}) async-start(), calls=%async_computation.2 | async-start | bytes 2621440 | tf_op jit(solution)/shard_map/all_gather | solution.py:27
  10.5 73.1 %collective-permute-start.14 = (s32[256]{0:T(256)S(1)}, s32[256]{0:T(256)S(1)}, u32[]{:S(2)}, u32[]{:S(2)}) collective-permute-start(s32[256]{0:T(256)S(1)} %copy-done.2), channel_id=1, source_target_pairs={{16,0},{20,4},{24,8},{28,12},{17,1},{21,5},{25,9},{29,13},{18,2},{... | collective-permute-start | bytes 3080 | tf_op jit(solution)/shard_map/ppermute | solution.py:12
  11.8 57.1 %collective-permute-start = (s32[256]{0:T(256)S(1)}, s32[256]{0:T(256)S(1)}, u32[]{:S(2)}, u32[]{:S(2)}) collective-permute-start(s32[256]{0:T(256)S(1)} %copy-done.2), channel_id=1, source_target_pairs={{0,4},{4,8},{8,12},{12,16},{16,20},{20,24},{24,28},{1,5},{5,9},{9,... | collective-permute-start | bytes 3080 | tf_op jit(solution)/shard_map/ppermute | solution.py:12
  14.2 47.7 %collective-permute-start.3 = (bf16[256,1024]{1,0:T(8,128)(2,1)}, bf16[256,1024]{1,0:T(8,128)(2,1)S(1)}, u32[]{:S(2)}, u32[]{:S(2)}) collective-permute-start(bf16[256,1024]{1,0:T(8,128)(2,1)} %fusion.2), channel_id=1, source_target_pairs={{4,0},{8,4},{12,8},{16,12},{20,16},{24,20},{28,24},{5,1},{9,5},{13... | collective-permute-start | bytes 1572872 | tf_op jit(solution)/shard_map/ppermute | solution.py:12
  15.5 54.7 %collective-permute-start.2 = (s32[256]{0:T(256)S(1)}, s32[256]{0:T(256)S(1)}, u32[]{:S(2)}, u32[]{:S(2)}) collective-permute-start(s32[256]{0:T(256)S(1)} %copy-done.2), channel_id=1, source_target_pairs={{4,0},{8,4},{12,8},{16,12},{20,16},{24,20},{28,24},{5,1},{9,5},{13... | collective-permute-start | bytes 3080 | tf_op jit(solution)/shard_map/ppermute | solution.py:12
  16.8 47.7 %collective-permute-start.5 = (bf16[256,1024]{1,0:T(8,128)(2,1)}, bf16[256,1024]{1,0:T(8,128)(2,1)S(1)}, u32[]{:S(2)}, u32[]{:S(2)}) collective-permute-start(bf16[256,1024]{1,0:T(8,128)(2,1)} %fusion.2), channel_id=1, source_target_pairs={{0,8},{4,12},{8,16},{12,20},{16,24},{20,28},{1,9},{5,13},{9,17},{1... | collective-permute-start | bytes 1572872 | tf_op jit(solution)/shard_map/ppermute | solution.py:12
  35.6 26.3 %copy-start.1 = (bf16[256,1024]{1,0:T(8,128)(2,1)S(1)}, bf16[256,1024]{1,0:T(8,128)(2,1)}, u32[]{:S(2)}) copy-start(bf16[256,1024]{1,0:T(8,128)(2,1)} %fusion.2) | copy-start | bytes 1572868
  59.3 4.4 %copy-start = (bf16[1024,1024]{1,0:T(8,128)(2,1)S(1)}, bf16[1024,1024]{1,0:T(8,128)(2,1)}, u32[]{:S(2)}) copy-start(bf16[1024,1024]{1,0:T(8,128)(2,1)} %all-gather.3.cloned.1.call-done) | copy-start | bytes 6291460
  61.9 14.8 %collective-permute-start.1 = (bf16[256,1024]{1,0:T(8,128)(2,1)S(1)}, bf16[256,1024]{1,0:T(8,128)(2,1)S(1)}, u32[]{:S(2)}, u32[]{:S(2)}) collective-permute-start(bf16[256,1024]{1,0:T(8,128)(2,1)S(1)} %copy-done.1), channel_id=1, source_target_pairs={{0,4},{4,8},{8,12},{12,16},{16,20},{20,24},{24,28},{1,5},{5,9},{9,... | collective-permute-start | bytes 1572872 | tf_op jit(solution)/shard_map/ppermute | solution.py:12
  64.5 7.0 %collective-permute-start.4 = (s32[256]{0:T(256)S(1)}, s32[256]{0:T(256)S(1)}, u32[]{:S(2)}, u32[]{:S(2)}) collective-permute-start(s32[256]{0:T(256)S(1)} %copy-done.2), channel_id=1, source_target_pairs={{0,8},{4,12},{8,16},{12,20},{16,24},{20,28},{1,9},{5,13},{9,17},{1... | collective-permute-start | bytes 3080 | tf_op jit(solution)/shard_map/ppermute | solution.py:12
  68.9 16.4 %collective-permute-start.15 = (bf16[256,1024]{1,0:T(8,128)(2,1)S(1)}, bf16[256,1024]{1,0:T(8,128)(2,1)S(1)}, u32[]{:S(2)}, u32[]{:S(2)}) collective-permute-start(bf16[256,1024]{1,0:T(8,128)(2,1)S(1)} %copy-done.1), channel_id=1, source_target_pairs={{16,0},{20,4},{24,8},{28,12},{17,1},{21,5},{25,9},{29,13},{18,2},{... | collective-permute-start | bytes 1572872 | tf_op jit(solution)/shard_map/ppermute | solution.py:12
  70.2 39.5 %collective-permute-start.6 = (s32[256]{0:T(256)S(1)}, s32[256]{0:T(256)S(1)}, u32[]{:S(2)}, u32[]{:S(2)}) collective-permute-start(s32[256]{0:T(256)S(1)} %copy-done.2), channel_id=1, source_target_pairs={{8,0},{12,4},{16,8},{20,12},{24,16},{28,20},{9,1},{13,5},{17,9},{2... | collective-permute-start | bytes 3080 | tf_op jit(solution)/shard_map/ppermute | solution.py:12
  71.5 16.1 %collective-permute-start.9 = (bf16[256,1024]{1,0:T(8,128)(2,1)S(1)}, bf16[256,1024]{1,0:T(8,128)(2,1)S(1)}, u32[]{:S(2)}, u32[]{:S(2)}) collective-permute-start(bf16[256,1024]{1,0:T(8,128)(2,1)S(1)} %copy-done.1), channel_id=1, source_target_pairs={{0,12},{4,16},{8,20},{12,24},{16,28},{1,13},{5,17},{9,21},{13,25},... | collective-permute-start | bytes 1572872 | tf_op jit(solution)/shard_map/ppermute | solution.py:12
  76.7 33.0 %collective-permute-start.8 = (s32[256]{0:T(256)S(1)}, s32[256]{0:T(256)S(1)}, u32[]{:S(2)}, u32[]{:S(2)}) collective-permute-start(s32[256]{0:T(256)S(1)} %copy-done.2), channel_id=1, source_target_pairs={{0,12},{4,16},{8,20},{12,24},{16,28},{1,13},{5,17},{9,21},{13,25},... | collective-permute-start | bytes 3080 | tf_op jit(solution)/shard_map/ppermute | solution.py:12
  83.6 10.5 %collective-permute-start.11 = (bf16[256,1024]{1,0:T(8,128)(2,1)S(1)}, bf16[256,1024]{1,0:T(8,128)(2,1)S(1)}, u32[]{:S(2)}, u32[]{:S(2)}) collective-permute-start(bf16[256,1024]{1,0:T(8,128)(2,1)S(1)} %copy-done.1), channel_id=1, source_target_pairs={{12,0},{16,4},{20,8},{24,12},{28,16},{13,1},{17,5},{21,9},{25,13},... | collective-permute-start | bytes 1572872 | tf_op jit(solution)/shard_map/ppermute | solution.py:12
  85.3 24.5 %collective-permute-start.10 = (s32[256]{0:T(256)S(1)}, s32[256]{0:T(256)S(1)}, u32[]{:S(2)}, u32[]{:S(2)}) collective-permute-start(s32[256]{0:T(256)S(1)} %copy-done.2), channel_id=1, source_target_pairs={{12,0},{16,4},{20,8},{24,12},{28,16},{13,1},{17,5},{21,9},{25,13},... | collective-permute-start | bytes 3080 | tf_op jit(solution)/shard_map/ppermute | solution.py:12
  87.6 16.9 %collective-permute-start.13 = (bf16[256,1024]{1,0:T(8,128)(2,1)S(1)}, bf16[256,1024]{1,0:T(8,128)(2,1)S(1)}, u32[]{:S(2)}, u32[]{:S(2)}) collective-permute-start(bf16[256,1024]{1,0:T(8,128)(2,1)S(1)} %copy-done.1), channel_id=1, source_target_pairs={{0,16},{4,20},{8,24},{12,28},{1,17},{5,21},{9,25},{13,29},{2,18},{... | collective-permute-start | bytes 1572872 | tf_op jit(solution)/shard_map/ppermute | solution.py:12
  94.1 16.1 %collective-permute-start.7 = (bf16[256,1024]{1,0:T(8,128)(2,1)S(1)}, bf16[256,1024]{1,0:T(8,128)(2,1)S(1)}, u32[]{:S(2)}, u32[]{:S(2)}) collective-permute-start(bf16[256,1024]{1,0:T(8,128)(2,1)S(1)} %copy-done.1), channel_id=1, source_target_pairs={{8,0},{12,4},{16,8},{20,12},{24,16},{28,20},{9,1},{13,5},{17,9},{2... | collective-permute-start | bytes 1572872 | tf_op jit(solution)/shard_map/ppermute | solution.py:12
  104.6 5.7 %collective-permute-start.12 = (s32[256]{0:T(256)S(1)}, s32[256]{0:T(256)S(1)}, u32[]{:S(2)}, u32[]{:S(2)}) collective-permute-start(s32[256]{0:T(256)S(1)} %copy-done.2), channel_id=1, source_target_pairs={{0,16},{4,20},{8,24},{12,28},{1,17},{5,21},{9,25},{13,29},{2,18},{... | collective-permute-start | bytes 3080 | tf_op jit(solution)/shard_map/ppermute | solution.py:12
  114.1 8.8 %all-to-all-start = ((f32[4,1,256]{2,1,0:T(1,128)}), f32[4,1,256]{2,1,0:T(1,128)S(1)}, u32[]{:S(2)}, u32[]{:S(2)}) async-start(f32[4,1,256]{2,1,0:T(1,128)} %bitcast.2), calls=%async_computation | async-start | bytes 8192 | tf_op jit(solution)/shard_map/all_to_all | solution.py:64
  122.9 8.8 %all-to-all-start.1 = ((f32[4,1,256]{2,1,0:T(1,128)}), f32[4,1,256]{2,1,0:T(1,128)S(1)}, u32[]{:S(2)}, u32[]{:S(2)}) async-start(f32[4,1,256]{2,1,0:T(1,128)} %bitcast.3), calls=%async_computation.1 | async-start | bytes 8192 | tf_op jit(solution)/shard_map/all_to_all | solution.py:67
Sparse Core Ops, SparseCore 0:
  10.6 48.6 all-gather.2
where the time goes:
time: 140 us; the launch traced here: 139 us
  starting transfers between devices  50.6 us (36%)
  waiting for transfers between devices  43.2 us (31%)
  between operations  14.4 us (10%)
  matrix products  14 us (10%)
  blocking collectives  11.3 us (8%)
  other arithmetic  5.68 us (4%)
    ppermute x16, starting transfers between devices, shifted(): return lax.ppermute(shard, axis, pairs)  44.1 us
    all_gather x1, waiting for transfers between devices, per_device(): lax.all_gather(unit, 'rep', axis=0, tiled=True)  23.7 us
    dot_general x9, matrix products, tile(): lax.dot_general(own, recv, (((1,), (1,)), ((), ())), preferred_element_ty...  14 us
    all_gather x1, blocking collectives, per_device(): lax.all_gather(cluster, 'rep', axis=0, tiled=True)  11.3 us
    ppermute x16, waiting for transfers between devices, shifted(): return lax.ppermute(shard, axis, pairs)  9.5 us
    all_to_all x1, waiting for transfers between devices, per_device(): lax.all_to_all(row_top.reshape(parts, quarter), 'rep', split_axis=0, conc...  4.96 us
    all_to_all x1, waiting for transfers between devices, per_device(): lax.all_to_all(row_mass.reshape(parts, quarter), 'rep', split_axis=0, con...  4.95 us
    all_to_all x1, starting transfers between devices, per_device(): lax.all_to_all(row_top.reshape(parts, quarter), 'rep', split_axis=0, conc...  3.24 us
  transfers between devices with their start and end apart: 19, of which 7 were waited for; matrix products, arithmetic and copies ran while one was open for 9% of the time, Pallas kernels for 0%

commit v1 on v0

v1 whole, which is shorter than its diff:
```python
import functools
import math

import jax
import jax.numpy as jnp
from jax import lax
from jax.experimental import pallas as pl
from jax.experimental.pallas import tpu as pltpu
from jax.sharding import PartitionSpec as P

MESH = pl.DeviceIdType.MESH
dup_scale = 8.0
LOG2 = dup_scale * math.log2(math.e)
NO_PAIR = -100.0
REACH = 3
SLOTS = 2 * REACH + 1
OWN, ZA, ZB = REACH, SLOTS, SLOTS + 1


def kernel(
    n, e_ref, c_ref, top_ref, mass_ref, buf, corner, xids, racc, cacc, rowres, rbuf, ssem, rsem
):
    q, width = e_ref.shape
    d = lax.axis_index("docs")
    z = lax.axis_index("rep")
    odd = lax.rem(d, 2)
    sister = d + 1 - 2 * odd
    to_a = jnp.where(z < 2, z + 2, 3 - z)
    from_a = jnp.where(z < 2, 3 - z, z - 2)
    mate = z + 1 - 2 * lax.rem(z, 2)
    inner = (z == 1) | (z == 2)
    outer = (z == 0) | (z == 3)

    def has(k):
        return (d + k >= 0) & (d + k < n)

    corner_in = (z == 0) & has(-4)
    corner_out = (z == 3) & has(4)

    def remote(src, dst, s, r, dev):
        return pltpu.make_async_remote_copy(
            src_ref=src,
            dst_ref=dst,
            send_sem=ssem.at[s],
            recv_sem=rsem.at[r],
            device_id=dev,
            device_id_type=MESH,
        )

    barrier = pltpu.get_barrier_semaphore()

    def greet(dev):
        pl.semaphore_signal(barrier, inc=1, device_id=dev, device_id_type=MESH)

    total = jnp.int32(3)
    for k in (-3, -2, -1, 1, 2, 3):
        pl.when(has(k))(functools.partial(greet, (d + k, z)))
        total = total + has(k).astype(jnp.int32)
    greet((d, to_a))
    greet((d, from_a))
    greet((d, mate))
    pl.when(corner_in)(functools.partial(greet, (d - 4, 3)))
    pl.when(corner_out)(functools.partial(greet, (d + 4, 0)))
    total = total + corner_in.astype(jnp.int32) + corner_out.astype(jnp.int32)

    x = e_ref[...].astype(jnp.float32)
    scale = lax.rsqrt(jnp.mean(x * x, axis=1, keepdims=True) + 1e-06)
    buf[OWN, 0:q, :] = (x * scale * width ** (-0.5)).astype(jnp.bfloat16)
    ids = c_ref[...].astype(jnp.float32)
    buf[OWN, q : q + 16, :] = jnp.zeros((16, width), jnp.bfloat16)
    buf[OWN, q : q + 16, 0:q] = jnp.broadcast_to(ids, (16, q)).astype(jnp.bfloat16)

    pl.semaphore_wait(barrier, total)

    own = buf.at[OWN]
    send_a = remote(own, buf.at[ZA], 6, ZA, (d, to_a))
    send_b = remote(own, buf.at[ZB], 7, ZB, (d, mate))
    send_p2 = remote(own, buf.at[REACH - 2], 1, REACH - 2, (d + 2, z))
    send_m2 = remote(own, buf.at[REACH + 2], 2, REACH + 2, (d - 2, z))
    sis_slot = REACH - 1 + 2 * odd
    send_sis = remote(own, buf.at[sis_slot], 0, sis_slot, (sister, z))
    far = 6 * odd - 3
    far_slot = REACH - far
    send_far = remote(own, buf.at[far_slot], 3, far_slot, (d + far, z))
    has_far = has(far)
    tail = pl.ds(q - 16, 32)
    send_corner = remote(buf.at[OWN, tail], corner, 8, SLOTS + 2, (d + 4, 0))

    pl.when(has(2))(send_p2.start)
    pl.when(has(-2))(send_m2.start)
    send_a.start()
    pl.when(outer)(send_b.start)
    send_sis.start()
    pl.when(has_far)(send_far.start)
    pl.when(corner_out)(send_corner.start)

    lanes = lax.broadcasted_iota(jnp.int32, (8, q), 1)
    subs = lax.broadcasted_iota(jnp.int32, (8, q), 0)

    def take_ids(slot):
        return buf[slot, q : q + 16, 0:q].astype(jnp.float32)[0:1]

    def load_x(slot, xi):
        row = jnp.broadcast_to(take_ids(slot), (128, q))
        xids[xi] = row.T
        racc[xi, 0] = jnp.full((q, 128), -1.0, jnp.float32)
        racc[xi, 1] = jnp.zeros((q, 128), jnp.float32)

    def tile(xslot, xi, slot, diagonal=False):
        scores = lax.dot_general(
            buf[xslot, 0:q, :],
            buf[slot, 0:q, :],
            (((1,), (1,)), ((), ())),
            preferred_element_type=jnp.float32,
        )
        yid = take_ids(slot)
        xid = xids[xi]
        tops, masses = [], []
        for lo in range(0, q, 128):
            mask = xid == yid[:, lo : lo + 128]
            if diagonal:
                i = lax.broadcasted_iota(jnp.int32, (q, 128), 0)
                j = lax.broadcasted_iota(jnp.int32, (q, 128), 1) + lo
                mask = mask & (i != j)
            top = jnp.where(mask, scores[:, lo : lo + 128], NO_PAIR)
            mass = jnp.exp2(top * LOG2 - LOG2)
            cols = pl.ds(lo, 128)
            cacc[slot, 0, :, cols] = jnp.maximum(
                cacc[slot, 0, :, cols], jnp.max(top.reshape(q // 8, 8, 128), axis=0)
            )
            cacc[slot, 1, :, cols] += jnp.sum(mass.reshape(q // 8, 8, 128), axis=0)
            tops.append(top)
            masses.append(mass)
        if not diagonal:
            racc[xi, 0] = jnp.maximum(racc[xi, 0], functools.reduce(jnp.maximum, tops))
            racc[xi, 1] += functools.reduce(jnp.add, masses)

    def row_result(xi):
        top = jnp.max(racc[xi, 0].T.reshape(16, 8, q), axis=0)
        mass = jnp.sum(racc[xi, 1].T.reshape(16, 8, q), axis=0)
        return top, mass

    cacc[:, 0] = jnp.full((SLOTS, 8, q), -1.0, jnp.float32)
    cacc[:, 1] = jnp.zeros((SLOTS, 8, q), jnp.float32)

    load_x(OWN, 0)
    tile(OWN, 0, OWN, diagonal=True)

    def arrived(slot):
        remote(own, buf.at[slot], 0, slot, (sister, z)).wait_recv()

    fwd_p2 = remote(
        buf.at[REACH + 2], buf.at[REACH + 1 + 2 * odd], 4, REACH + 1 + 2 * odd, (sister, z)
    )
    fwd_m2 = remote(
        buf.at[REACH - 2], buf.at[REACH - 3 + 2 * odd], 5, REACH - 3 + 2 * odd, (sister, z)
    )

    @pl.when(has(2))
    def _():
        arrived(REACH + 2)
        fwd_p2.start()

    @pl.when(has(-2))
    def _():
        arrived(REACH - 2)
        fwd_m2.start()

    for k in (1, -1, 3, -3):
        pl.when(has(k))(functools.partial(arrived, REACH + k))

    def own_step(slot, carry):
        @pl.when(has(slot - REACH))
        def _():
            tile(OWN, 0, slot)

        return carry

    lax.fori_loop(OWN + 1, SLOTS, own_step, 0)

    def other_quarter(xslot, xi, s, r, dev):
        arrived(xslot)
        load_x(xslot, xi)

        def step(slot, carry):
            @pl.when(has(slot - REACH))
            def _():
                tile(xslot, xi, slot)

            return carry

        lax.fori_loop(0, SLOTS, step, 0)
        top, mass = row_result(xi)
        rowres[xi - 1, 0] = top
        rowres[xi - 1, 1] = mass
        remote(rowres.at[xi - 1], rbuf.at[r], s, SLOTS + 3 + r, dev).start()

    @pl.when(inner)
    def _():
        other_quarter(ZB, 2, 17, ZB, (d, mate))

    other_quarter(ZA, 1, 16, ZA, (d, from_a))

    back = remote(rowres.at[2], rbuf.at[SLOTS + 2], 18, 2 * SLOTS + 5, (d - 4, 3))

    @pl.when(corner_in)
    def _():
        remote(buf.at[OWN, tail], corner, 8, SLOTS + 2, (d - 4, 3)).wait_recv()
        first = buf[OWN, 0:16, :].astype(jnp.float32)[0:1]
        last = corner[0:16, :].astype(jnp.float32)[15:16]
        cos = jnp.sum(first * last, axis=1, keepdims=True)
        here = take_ids(OWN)[:, 0:1]
        there = corner[16:32, 0:q].astype(jnp.float32)[0:1, q - 1 : q]
        top = jnp.broadcast_to(jnp.where(here == there, cos, NO_PAIR), (8, q))
        mass = jnp.exp2(top * LOG2 - LOG2)
        mine = (lanes == 0) & (subs == 0)
        cacc[OWN, 0] = jnp.maximum(cacc[OWN, 0], jnp.where(mine, top, -1.0))
        cacc[OWN, 1] += jnp.where(mine, mass, 0.0)
        theirs = (lanes == q - 1) & (subs == 0)
        rowres[2, 0] = jnp.where(theirs, top, -1.0)
        rowres[2, 1] = jnp.where(theirs, mass, 0.0)
        back.start()

    def result(k):
        return remote(
            cacc.at[REACH + k],
            rbuf.at[REACH - k],
            9 + REACH + k,
            SLOTS + 3 + REACH - k,
            (d + k, z),
        )

    for k in (-3, -2, -1, 1, 2, 3):
        pl.when(has(k))(result(k).start)

    top, mass = row_result(0)
    top_ref[...] = jnp.max(jnp.maximum(top, cacc[OWN, 0]), axis=0, keepdims=True)
    mass_ref[...] = jnp.sum(mass + cacc[OWN, 1], axis=0, keepdims=True)

    def add_result(slot):
        remote(rowres.at[0], rbuf.at[slot], 16, SLOTS + 3 + slot, (sister, z)).wait_recv()
        top_ref[...] = jnp.maximum(
            top_ref[...], jnp.max(rbuf[slot, 0], axis=0, keepdims=True)
        )
        mass_ref[...] += jnp.sum(rbuf[slot, 1], axis=0, keepdims=True)

    pl.when(corner_out)(functools.partial(add_result, SLOTS + 2))
    for k in (-3, -2, -1, 1, 2, 3):
        pl.when(has(k))(functools.partial(add_result, REACH + k))
    add_result(ZA)
    pl.when(outer)(functools.partial(add_result, ZB))

    pl.when(has(2))(send_p2.wait_send)
    pl.when(has(-2))(send_m2.wait_send)
    send_a.wait_send()
    pl.when(outer)(send_b.wait_send)
    send_sis.wait_send()
    pl.when(has_far)(send_far.wait_send)
    pl.when(corner_out)(send_corner.wait_send)
    pl.when(has(2))(fwd_p2.wait_send)
    pl.when(has(-2))(fwd_m2.wait_send)
    for k in (-3, -2, -1, 1, 2, 3):
        pl.when(has(k))(result(k).wait_send)
    remote(rowres.at[0], rbuf.at[ZA], 16, SLOTS + 3 + ZA, (d, from_a)).wait_send()

    @pl.when(inner)
    def _():
        remote(rowres.at[1], rbuf.at[ZB], 17, SLOTS + 3 + ZB, (d, mate)).wait_send()

    pl.when(corner_in)(back.wait_send)


def per_device(n, embeds, cluster):
    q, width = embeds.shape
    top, mass = pl.pallas_call(
        functools.partial(kernel, n),
        out_shape=(jax.ShapeDtypeStruct((1, q), jnp.float32),) * 2,
        in_specs=[pl.BlockSpec(memory_space=pltpu.VMEM)] * 2,
        out_specs=(pl.BlockSpec(memory_space=pltpu.VMEM),) * 2,
        scratch_shapes=[
            pltpu.VMEM((SLOTS + 2, q + 16, width), jnp.bfloat16),
            pltpu.VMEM((32, width), jnp.bfloat16),
            pltpu.VMEM((3, q, 128), jnp.float32),
            pltpu.VMEM((3, 2, q, 128), jnp.float32),
            pltpu.VMEM((SLOTS, 2, 8, q), jnp.float32),
            pltpu.VMEM((3, 2, 8, q), jnp.float32),
            pltpu.VMEM((SLOTS + 3, 2, 8, q), jnp.float32),
            pltpu.SemaphoreType.DMA((19,)),
            pltpu.SemaphoreType.DMA((2 * SLOTS + 6,)),
        ],
        compiler_params=pltpu.CompilerParams(
            collective_id=0, has_side_effects=True, vmem_limit_bytes=32 * 2**20
        ),
        name="dedup",
    )(embeds, cluster.reshape(1, q))
    return top.reshape(q), mass.reshape(q)


def solution(mesh):
    return jax.shard_map(
        functools.partial(per_device, mesh.shape["docs"]),
        mesh=mesh,
        in_specs=(P(("docs", "rep"), None), P(("docs", "rep"))),
        out_specs=(P(("docs", "rep")), P(("docs", "rep"))),
        check_vma=False,
    )
```

time: 140 us -> 45.1 us (0.32)
  the two profiles are of different devices: /device:TPU:0 before, /device:TPU:13 now
where the time goes in v1:
time: 45.1 us; the launch traced here: 44.9 us
  Pallas kernels  41.5 us (92%)
  local copies, waits for them, and re-layouts  2.84 us (6%)
  between operations  0.65 us (1%)
    pallas_call x1, Pallas kernels, per_device(): pl.pallas_call(functools.partial(kernel, n), out_shape=(jax.ShapeDtypeStr...  41.5 us
    unnamed x6, local copies, waits for them, and re-layouts  2.84 us

profile of v1, /device:TPU:13, one launch (start us, length us, event | category | flops | bytes accessed | tf_op | source)
XLA Modules:
  0.0 44.9 jit_solution(17749910147027284212)
XLA Ops:
  0.6 0.0 copy-start.1
  0.6 0.7 %copy-done.1 = s32[256]{0:T(256)S(1)} copy-done((s32[256]{0:T(256)S(1)}, s32[256]{0:T(256)}, u32[]{:S(2)}) %copy-start.1) | copy-done | bytes 1048
  1.3 0.0 copy-start
  1.3 1.0 %copy-done = bf16[256,1024]{1,0:T(8,128)(2,1)S(1)} copy-done((bf16[256,1024]{1,0:T(8,128)(2,1)S(1)}, bf16[256,1024]{1,0:T(8,128)(2,1)}, u32[]{:S(2)}) %copy-start) | copy-done | bytes 524312
  2.4 41.5 %dedup.1 = (f32[1,256]{1,0:T(1,128)S(1)}, f32[1,256]{1,0:T(1,128)S(1)}) custom-call(bf16[256,1024]{1,0:T(8,128)(2,1)S(1)} %copy-done, s32[1,256]{1,0:T(1,128)S(1)} %bitcast.3), custom_call_target="tpu_custom_call" | custom-call | tf_op jit(solution)/shard_map/dedup/pallas_call | solution.py:275
  43.8 0.6 %copy.6 = f32[256]{0:T(256)} copy(f32[256]{0:T(256)S(1)} %bitcast.5) | data formatting | bytes 2048
  44.4 0.6 %copy.7 = f32[256]{0:T(256)} copy(f32[256]{0:T(256)S(1)} %bitcast.4) | data formatting | bytes 2048
Async XLA Ops:
  0.6 0.7 %copy-start.1 = (s32[256]{0:T(256)S(1)}, s32[256]{0:T(256)}, u32[]{:S(2)}) copy-start(s32[256]{0:T(256)} %param.3) | copy-start | bytes 3076
  1.3 1.0 %copy-start = (bf16[256,1024]{1,0:T(8,128)(2,1)S(1)}, bf16[256,1024]{1,0:T(8,128)(2,1)}, u32[]{:S(2)}) copy-start(bf16[256,1024]{1,0:T(8,128)(2,1)} %e_ref.1) | copy-start | bytes 1572868

commit v2 on v1

v2 whole, which is shorter than its diff:
```python
import functools
import math

import jax
import jax.numpy as jnp
from jax import lax
from jax.experimental import pallas as pl
from jax.experimental.pallas import tpu as pltpu
from jax.sharding import PartitionSpec as P

MESH = pl.DeviceIdType.MESH
dup_scale = 8.0
LOG2 = dup_scale * math.log2(math.e)
NO_PAIR = -100.0
REACH = 3
SLOTS = 2 * REACH + 1
OWN, ZA, ZB = REACH, SLOTS, SLOTS + 1
S_RES = 10
S_Z = S_RES + SLOTS
R_CORNER = SLOTS
R_RES = R_CORNER + 1
R_Z = R_RES + SLOTS + 3


def kernel(
    n,
    e_hbm,
    c_hbm,
    top_ref,
    mass_ref,
    e_ref,
    c_ref,
    buf,
    corner,
    xids,
    racc,
    cacc,
    rowres,
    rbuf,
    ssem,
    rsem,
    lsem,
):
    q, width = e_ref.shape
    half = q // 2
    d = lax.axis_index("docs")
    z = lax.axis_index("rep")
    odd = lax.rem(d, 2)
    corner_of_four = lax.rem(d, 4)
    low = corner_of_four < 2
    sis = 1 - 2 * odd
    near = jnp.where(low, 2, -2)
    far = 6 * odd - 3
    sister = d + sis
    to_a = jnp.where(z < 2, z + 2, 3 - z)
    from_a = jnp.where(z < 2, 3 - z, z - 2)
    mate = z + 1 - 2 * lax.rem(z, 2)
    inner = (z == 1) | (z == 2)
    outer = (z == 0) | (z == 3)

    def has(k):
        return (d + k >= 0) & (d + k < n)

    corner_in = (z == 0) & has(-4)
    corner_out = (z == 3) & has(4)
    ends = (corner_of_four == 0) | (corner_of_four == 3)

    def remote(src, dst, s, r, dev):
        return pltpu.make_async_remote_copy(
            src_ref=src,
            dst_ref=dst,
            send_sem=ssem.at[s],
            recv_sem=rsem.at[r],
            device_id=dev,
            device_id_type=MESH,
        )

    barrier = pltpu.get_barrier_semaphore()

    def greet(dev):
        pl.semaphore_signal(barrier, inc=1, device_id=dev, device_id_type=MESH)

    load_e = pltpu.make_async_copy(e_hbm, e_ref, lsem.at[0])
    load_c = pltpu.make_async_copy(c_hbm, c_ref, lsem.at[1])
    load_e.start()
    load_c.start()
    total = jnp.int32(3)
    for k in (-3, -2, -1, 1, 2, 3):
        pl.when(has(k))(functools.partial(greet, (d + k, z)))
        total = total + has(k).astype(jnp.int32)
    for k in (-4, 4):
        pl.when(has(k) & ends)(functools.partial(greet, (d + k, z)))
        total = total + (has(k) & ends).astype(jnp.int32)
    greet((d, to_a))
    greet((d, from_a))
    greet((d, mate))
    pl.when(corner_in)(functools.partial(greet, (d - 4, 3)))
    pl.when(corner_out)(functools.partial(greet, (d + 4, 0)))
    total = total + corner_in.astype(jnp.int32) + corner_out.astype(jnp.int32)

    own = buf.at[OWN]
    id_rows = pl.ds(q, 16)

    def z_copy(part, slot, dev):
        first = 3 * (slot - ZA)
        if part == 2:
            view = (id_rows, pl.ds(0, q))
        else:
            view = (pl.ds(part * half, half),)
        return remote(
            buf.at[(OWN,) + view],
            buf.at[(slot,) + view],
            S_Z + first + part,
            R_Z + first + part,
            dev,
        )

    def send_z(part):
        z_copy(part, ZA, (d, to_a)).start()
        pl.when(outer)(z_copy(part, ZB, (d, mate)).start)

    load_c.wait()
    ids = c_ref[...].astype(jnp.float32)
    buf[OWN, q : q + 16, :] = jnp.zeros((16, width), jnp.bfloat16)
    buf[OWN, q : q + 16, 0:q] = jnp.broadcast_to(ids, (16, q)).astype(jnp.bfloat16)
    load_e.wait()
    for part in range(2):
        rows = pl.ds(part * half, half)
        x = e_ref[rows, :].astype(jnp.float32)
        scale = lax.rsqrt(jnp.mean(x * x, axis=1, keepdims=True) + 1e-06)
        buf[OWN, rows, :] = (x * scale * width ** (-0.5)).astype(jnp.bfloat16)
        if part == 0:
            pl.semaphore_wait(barrier, total)
            send_z(2)
        send_z(part)

    send_near = remote(own, buf.at[REACH - near], 0, REACH - near, (d + near, z))
    send_far = remote(own, buf.at[REACH - far], 1, REACH - far, (d + far, z))
    send_sis = remote(own, buf.at[REACH - sis], 2, REACH - sis, (sister, z))
    has_far = has(far)
    tail = pl.ds(q - 16, 32)
    send_corner = remote(buf.at[OWN, tail], corner, 3, R_CORNER, (d + 4, 0))
    pl.when(has_far)(send_far.start)
    send_near.start()
    send_sis.start()
    pl.when(corner_out)(send_corner.start)

    lanes = lax.broadcasted_iota(jnp.int32, (8, q), 1)
    subs = lax.broadcasted_iota(jnp.int32, (8, q), 0)

    def take_ids(slot):
        return buf[slot, q : q + 16, 0:q].astype(jnp.float32)[0:1]

    def load_x(slot):
        xids[...] = jnp.broadcast_to(take_ids(slot), (128, q)).T

    def clear_rows():
        racc[0] = jnp.full((q, 128), -1.0, jnp.float32)
        racc[1] = jnp.zeros((q, 128), jnp.float32)

    def tile(xslot, start, size, slot, diagonal=False):
        rows = pl.ds(start, size)
        scores = lax.dot_general(
            buf[xslot, rows, :],
            buf[slot, 0:q, :],
            (((1,), (1,)), ((), ())),
            preferred_element_type=jnp.float32,
        )
        yid = take_ids(slot)
        xid = xids[rows, :]
        tops, masses = [], []
        for lo in range(0, q, 128):
            mask = xid == yid[:, lo : lo + 128]
            if diagonal:
                i = lax.broadcasted_iota(jnp.int32, (size, 128), 0)
                j = lax.broadcasted_iota(jnp.int32, (size, 128), 1) + lo
                mask = mask & (i != j)
            top = jnp.where(mask, scores[:, lo : lo + 128], NO_PAIR)
            mass = jnp.exp2(top * LOG2 - LOG2)
            cols = pl.ds(lo, 128)
            cacc[slot, 0, :, cols] = jnp.maximum(
                cacc[slot, 0, :, cols], jnp.max(top.reshape(size // 8, 8, 128), axis=0)
            )
            cacc[slot, 1, :, cols] += jnp.sum(mass.reshape(size // 8, 8, 128), axis=0)
            tops.append(top)
            masses.append(mass)
        if not diagonal:
            racc[0, rows, :] = jnp.maximum(racc[0, rows, :], functools.reduce(jnp.maximum, tops))
            racc[1, rows, :] += functools.reduce(jnp.add, masses)

    def row_result(xi, start, size):
        rows = pl.ds(start, size)
        rowres[xi, 0, :, rows] = jnp.max(racc[0, rows, :].T.reshape(16, 8, size), axis=0)
        rowres[xi, 1, :, rows] = jnp.sum(racc[1, rows, :].T.reshape(16, 8, size), axis=0)

    cacc[:, 0] = jnp.full((SLOTS, 8, q), -1.0, jnp.float32)
    cacc[:, 1] = jnp.zeros((SLOTS, 8, q), jnp.float32)

    load_x(OWN)
    clear_rows()
    tile(OWN, 0, q, OWN, diagonal=True)

    def arrived(slot):
        remote(own, buf.at[slot], 0, slot, (sister, z)).wait_recv()

    across = jnp.where(low, 4 - 3 * odd, -1 - 3 * odd)
    across_from = jnp.where(low, 2 + odd, -3 + odd)
    has_across = has(across) & has(across_from)

    def go_on(slot, s, by):
        to = slot - by
        return remote(buf.at[slot], buf.at[to], s, to, (d + by, z))

    go_across = go_on(REACH + across_from, 4, across)
    go_near = go_on(REACH + near, 5, sis)
    go_diag = go_on(REACH - near, 6, sis)
    has_diag = has(-near)

    @pl.when(has_far)
    def _():
        arrived(REACH + far)

    pl.when(has_across & jnp.logical_not(ends))(go_across.start)
    arrived(REACH + near)
    go_near.start()
    pl.when(has_across & ends)(go_across.start)
    arrived(REACH + sis)

    order = (0, sis, near, far, near + sis, -near, -near + sis)

    def nth(i):
        k = jnp.int32(0)
        for j in range(1, SLOTS):
            k = jnp.where(i == j, order[j], k)
        return k

    def own_step(i, carry):
        k = nth(i)

        @pl.when((k > 0) & has(k))
        def _():
            tile(OWN, 0, q, REACH + k)

        return carry

    lax.fori_loop(1, 4, own_step, 0)

    @pl.when(has_diag)
    def _():
        arrived(REACH - near)
        go_diag.start()

    pl.when(has(near + sis))(functools.partial(arrived, REACH + near + sis))
    pl.when(has(-near + sis))(functools.partial(arrived, REACH - near + sis))
    lax.fori_loop(4, SLOTS, own_step, 0)
    row_result(0, 0, q)
    clear_rows()

    def other_half(slot, xi, part, dev):
        if part == 0:
            z_copy(2, slot, dev).wait_recv()
        load_x(slot)
        z_copy(part, slot, dev).wait_recv()

        def step(i, carry):
            @pl.when(has(i - REACH))
            def _():
                tile(slot, part * half, half, i)

            return carry

        lax.fori_loop(0, SLOTS, step, 0)
        row_result(xi, part * half, half)

    row_a = remote(rowres.at[1], rbuf.at[ZA], 7, R_RES + ZA, (d, from_a))
    row_b = remote(rowres.at[2], rbuf.at[ZB], 8, R_RES + ZB, (d, mate))

    other_half(ZA, 1, 0, (d, from_a))

    @pl.when(inner)
    def _():
        clear_rows()
        other_half(ZB, 2, 0, (d, mate))
        other_half(ZB, 2, 1, (d, mate))
        row_b.start()
        clear_rows()

    other_half(ZA, 1, 1, (d, from_a))
    row_a.start()

    back = remote(rowres.at[3], rbuf.at[SLOTS + 2], 9, R_RES + SLOTS + 2, (d - 4, 3))

    @pl.when(corner_in)
    def _():
        remote(buf.at[OWN, tail], corner, 3, R_CORNER, (d - 4, 3)).wait_recv()
        first = buf[OWN, 0:16, :].astype(jnp.float32)[0:1]
        last = corner[0:16, :].astype(jnp.float32)[15:16]
        cos = jnp.sum(first * last, axis=1, keepdims=True)
        here = take_ids(OWN)[:, 0:1]
        there = corner[16:32, 0:q].astype(jnp.float32)[0:1, q - 1 : q]
        top = jnp.broadcast_to(jnp.where(here == there, cos, NO_PAIR), (8, q))
        mass = jnp.exp2(top * LOG2 - LOG2)
        mine = (lanes == 0) & (subs == 0)
        cacc[OWN, 0] = jnp.maximum(cacc[OWN, 0], jnp.where(mine, top, -1.0))
        cacc[OWN, 1] += jnp.where(mine, mass, 0.0)
        theirs = (lanes == q - 1) & (subs == 0)
        rowres[3, 0] = jnp.where(theirs, top, -1.0)
        rowres[3, 1] = jnp.where(theirs, mass, 0.0)
        back.start()

    def result(k):
        return remote(
            cacc.at[REACH + k],
            rbuf.at[REACH - k],
            S_RES + REACH + k,
            R_RES + REACH - k,
            (d + k, z),
        )

    for k in (-3, -2, -1, 1, 2, 3):
        pl.when(has(k))(result(k).start)

    top_ref[...] = jnp.max(jnp.maximum(rowres[0, 0], cacc[OWN, 0]), axis=0, keepdims=True)
    mass_ref[...] = jnp.sum(rowres[0, 1] + cacc[OWN, 1], axis=0, keepdims=True)

    def add_result(slot):
        remote(rowres.at[0], rbuf.at[slot], 7, R_RES + slot, (sister, z)).wait_recv()
        top_ref[...] = jnp.maximum(
            top_ref[...], jnp.max(rbuf[slot, 0], axis=0, keepdims=True)
        )
        mass_ref[...] += jnp.sum(rbuf[slot, 1], axis=0, keepdims=True)

    pl.when(corner_out)(functools.partial(add_result, SLOTS + 2))
    for k in (-3, -2, -1, 1, 2, 3):
        pl.when(has(k))(functools.partial(add_result, REACH + k))
    add_result(ZA)
    pl.when(outer)(functools.partial(add_result, ZB))

    for part in range(3):
        z_copy(part, ZA, (d, to_a)).wait_send()
        pl.when(outer)(z_copy(part, ZB, (d, mate)).wait_send)
    send_near.wait_send()
    pl.when(has_far)(send_far.wait_send)
    send_sis.wait_send()
    pl.when(corner_out)(send_corner.wait_send)
    pl.when(has_across)(go_across.wait_send)
    go_near.wait_send()
    pl.when(has_diag)(go_diag.wait_send)
    for k in (-3, -2, -1, 1, 2, 3):
        pl.when(has(k))(result(k).wait_send)
    row_a.wait_send()
    pl.when(inner)(row_b.wait_send)
    pl.when(corner_in)(back.wait_send)


def per_device(n, embeds, cluster):
    q, width = embeds.shape
    top, mass = pl.pallas_call(
        functools.partial(kernel, n),
        out_shape=(jax.ShapeDtypeStruct((1, q), jnp.float32),) * 2,
        in_specs=[pl.BlockSpec(memory_space=pltpu.HBM)] * 2,
        out_specs=(pl.BlockSpec(memory_space=pltpu.VMEM),) * 2,
        scratch_shapes=[
            pltpu.VMEM((q, width), jnp.bfloat16),
            pltpu.VMEM((1, q), jnp.int32),
            pltpu.VMEM((SLOTS + 2, q + 16, width), jnp.bfloat16),
            pltpu.VMEM((32, width), jnp.bfloat16),
            pltpu.VMEM((q, 128), jnp.float32),
            pltpu.VMEM((2, q, 128), jnp.float32),
            pltpu.VMEM((SLOTS, 2, 8, q), jnp.float32),
            pltpu.VMEM((4, 2, 8, q), jnp.float32),
            pltpu.VMEM((SLOTS + 3, 2, 8, q), jnp.float32),
            pltpu.SemaphoreType.DMA((S_Z + 6,)),
            pltpu.SemaphoreType.DMA((R_Z + 6,)),
            pltpu.SemaphoreType.DMA((2,)),
        ],
        compiler_params=pltpu.CompilerParams(
            collective_id=0, has_side_effects=True, vmem_limit_bytes=32 * 2**20
        ),
        name="dedup",
    )(embeds, cluster.reshape(1, q))
    return top.reshape(q), mass.reshape(q)


def solution(mesh):
    return jax.shard_map(
        functools.partial(per_device, mesh.shape["docs"]),
        mesh=mesh,
        in_specs=(P(("docs", "rep"), None), P(("docs", "rep"))),
        out_specs=(P(("docs", "rep")), P(("docs", "rep"))),
        check_vma=False,
    )
```

time: 45.1 us -> 43.6 us (0.967)
  the two profiles are of different devices: /device:TPU:13 before, /device:TPU:5 now
where the time goes in v2:
time: 43.6 us; the launch traced here: 43.4 us
  Pallas kernels  39.9 us (92%)
  local copies, waits for them, and re-layouts  2.84 us (7%)
  between operations  0.65 us (1%)
    pallas_call x1, Pallas kernels, per_device(): pl.pallas_call(functools.partial(kernel, n), out_shape=(jax.ShapeDtypeStr...  39.9 us
    unnamed x6, local copies, waits for them, and re-layouts  2.84 us

profile of v2, /device:TPU:5, one launch (start us, length us, event | category | flops | bytes accessed | tf_op | source)
XLA Modules:
  0.0 43.4 jit_solution(15872432137551334258)
XLA Ops:
  0.6 0.0 copy-start.1
  0.6 0.7 %copy-done.1 = s32[256]{0:T(256)S(1)} copy-done((s32[256]{0:T(256)S(1)}, s32[256]{0:T(256)}, u32[]{:S(2)}) %copy-start.1) | copy-done | bytes 1048
  1.3 0.0 copy-start
  1.3 1.0 %copy-done = bf16[256,1024]{1,0:T(8,128)(2,1)S(1)} copy-done((bf16[256,1024]{1,0:T(8,128)(2,1)S(1)}, bf16[256,1024]{1,0:T(8,128)(2,1)}, u32[]{:S(2)}) %copy-start) | copy-done | bytes 524312
  2.4 39.9 %dedup.1 = (f32[1,256]{1,0:T(1,128)S(1)}, f32[1,256]{1,0:T(1,128)S(1)}) custom-call(bf16[256,1024]{1,0:T(8,128)(2,1)S(1)} %copy-done, s32[1,256]{1,0:T(1,128)S(1)} %bitcast.3), custom_call_target="tpu_custom_call" | custom-call | tf_op jit(solution)/shard_map/dedup/pallas_call | solution.py:358
  42.3 0.6 %copy.6 = f32[256]{0:T(256)} copy(f32[256]{0:T(256)S(1)} %bitcast.5) | data formatting | bytes 2048
  42.8 0.6 %copy.7 = f32[256]{0:T(256)} copy(f32[256]{0:T(256)S(1)} %bitcast.4) | data formatting | bytes 2048
Async XLA Ops:
  0.6 0.7 %copy-start.1 = (s32[256]{0:T(256)S(1)}, s32[256]{0:T(256)}, u32[]{:S(2)}) copy-start(s32[256]{0:T(256)} %param.3) | copy-start | bytes 3076
  1.3 1.0 %copy-start = (bf16[256,1024]{1,0:T(8,128)(2,1)S(1)}, bf16[256,1024]{1,0:T(8,128)(2,1)}, u32[]{:S(2)}) copy-start(bf16[256,1024]{1,0:T(8,128)(2,1)} %e_hbm.1) | copy-start | bytes 1572868

commit v3 on v2

--- a/solution.py
+++ b/solution.py
@@ -15,9 +15,11 @@
 REACH = 3
 SLOTS = 2 * REACH + 1
 OWN, ZA, ZB = REACH, SLOTS, SLOTS + 1
-S_RES = 10
+S_CORNER = 12
+S_ROW = S_CORNER + 1
+S_RES = S_ROW + 3
 S_Z = S_RES + SLOTS
-R_CORNER = SLOTS
+R_CORNER = 2 * SLOTS
 R_RES = R_CORNER + 1
 R_Z = R_RES + SLOTS + 3
 
@@ -98,7 +100,6 @@
     pl.when(corner_out)(functools.partial(greet, (d + 4, 0)))
     total = total + corner_in.astype(jnp.int32) + corner_out.astype(jnp.int32)
 
-    own = buf.at[OWN]
     id_rows = pl.ds(q, 16)
 
     def z_copy(part, slot, dev):
@@ -116,8 +117,21 @@
         )
 
     def send_z(part):
+        pl.when(outer)(z_copy(part, ZB, (d, mate)).start)
         z_copy(part, ZA, (d, to_a)).start()
-        pl.when(outer)(z_copy(part, ZB, (d, mate)).start)
+
+    def halves(slot, to, s, dev):
+        return [
+            remote(buf.at[slot, view], buf.at[to, view], 2 * s + part, 2 * to + part, dev)
+            for part, view in enumerate((pl.ds(0, half), pl.ds(half, half + 16)))
+        ]
+
+    send_near = halves(OWN, REACH - near, 0, (d + near, z))
+    send_far = halves(OWN, REACH - far, 1, (d + far, z))
+    send_sis = halves(OWN, REACH - sis, 2, (sister, z))
+    has_far = has(far)
+    tail = pl.ds(q - 16, 32)
+    send_corner = remote(buf.at[OWN, tail], corner, S_CORNER, R_CORNER, (d + 4, 0))
 
     load_c.wait()
     ids = c_ref[...].astype(jnp.float32)
@@ -131,18 +145,12 @@
         buf[OWN, rows, :] = (x * scale * width ** (-0.5)).astype(jnp.bfloat16)
         if part == 0:
             pl.semaphore_wait(barrier, total)
+        pl.when(has_far)(send_far[part].start)
+        send_near[part].start()
+        send_z(part)
+        send_sis[part].start()
+        if part == 0:
             send_z(2)
-        send_z(part)
-
-    send_near = remote(own, buf.at[REACH - near], 0, REACH - near, (d + near, z))
-    send_far = remote(own, buf.at[REACH - far], 1, REACH - far, (d + far, z))
-    send_sis = remote(own, buf.at[REACH - sis], 2, REACH - sis, (sister, z))
-    has_far = has(far)
-    tail = pl.ds(q - 16, 32)
-    send_corner = remote(buf.at[OWN, tail], corner, 3, R_CORNER, (d + 4, 0))
-    pl.when(has_far)(send_far.start)
-    send_near.start()
-    send_sis.start()
     pl.when(corner_out)(send_corner.start)
 
     lanes = lax.broadcasted_iota(jnp.int32, (8, q), 1)
@@ -200,30 +208,29 @@
     clear_rows()
     tile(OWN, 0, q, OWN, diagonal=True)
 
-    def arrived(slot):
-        remote(own, buf.at[slot], 0, slot, (sister, z)).wait_recv()
+    def arrived(slot, parts=(0, 1)):
+        copies = halves(OWN, slot, 0, (sister, z))
+        for part in parts:
+            copies[part].wait_recv()
 
     across = jnp.where(low, 4 - 3 * odd, -1 - 3 * odd)
     across_from = jnp.where(low, 2 + odd, -3 + odd)
     has_across = has(across) & has(across_from)
 
     def go_on(slot, s, by):
-        to = slot - by
-        return remote(buf.at[slot], buf.at[to], s, to, (d + by, z))
-
-    go_across = go_on(REACH + across_from, 4, across)
-    go_near = go_on(REACH + near, 5, sis)
-    go_diag = go_on(REACH - near, 6, sis)
+        return halves(slot, slot - by, s, (d + by, z))
+
+    go_across = go_on(REACH + across_from, 3, across)
+    go_near = go_on(REACH + near, 4, sis)
+    go_diag = go_on(REACH - near, 5, sis)
     has_diag = has(-near)
 
-    @pl.when(has_far)
-    def _():
-        arrived(REACH + far)
-
-    pl.when(has_across & jnp.logical_not(ends))(go_across.start)
-    arrived(REACH + near)
-    go_near.start()
-    pl.when(has_across & ends)(go_across.start)
+    for part in range(2):
+        pl.when(has_far)(functools.partial(arrived, REACH + far, (part,)))
+        pl.when(has_across & jnp.logical_not(ends))(go_across[part].start)
+        arrived(REACH + near, (part,))
+        pl.when(has_across & ends)(go_across[part].start)
+        go_near[part].start()
     arrived(REACH + sis)
 
     order = (0, sis, near, far, near + sis, -near, -near + sis)
@@ -247,8 +254,9 @@
 
     @pl.when(has_diag)
     def _():
-        arrived(REACH - near)
-        go_diag.start()
+        for part in range(2):
+            arrived(REACH - near, (part,))
+            go_diag[part].start()
 
     pl.when(has(near + sis))(functools.partial(arrived, REACH + near + sis))
     pl.when(has(-near + sis))(functools.partial(arrived, REACH - near + sis))
@@ -256,43 +264,55 @@
     row_result(0, 0, q)
     clear_rows()
 
-    def other_half(slot, xi, part, dev):
+    def result(k):
+        return remote(
+            cacc.at[REACH + k],
+            rbuf.at[REACH - k],
+            S_RES + REACH + k,
+            R_RES + REACH - k,
+            (d + k, z),
+        )
+
+    def other_half(slot, xi, part, xz, dev, last=False):
         if part == 0:
             z_copy(2, slot, dev).wait_recv()
         load_x(slot)
         z_copy(part, slot, dev).wait_recv()
 
         def step(i, carry):
-            @pl.when(has(i - REACH))
+            k = i - REACH
+            apart = ((k == REACH) & (xz < z - 1)) | ((k == -REACH) & (z < xz - 1))
+
+            @pl.when(has(k) & jnp.logical_not(apart))
             def _():
                 tile(slot, part * half, half, i)
 
+            if last:
+                pl.when(has(k) & (k != 0))(lambda: result(k).start())
             return carry
 
         lax.fori_loop(0, SLOTS, step, 0)
         row_result(xi, part * half, half)
 
-    row_a = remote(rowres.at[1], rbuf.at[ZA], 7, R_RES + ZA, (d, from_a))
-    row_b = remote(rowres.at[2], rbuf.at[ZB], 8, R_RES + ZB, (d, mate))
-
-    other_half(ZA, 1, 0, (d, from_a))
+    row_a = remote(rowres.at[1], rbuf.at[ZA], S_ROW, R_RES + ZA, (d, from_a))
+    row_b = remote(rowres.at[2], rbuf.at[ZB], S_ROW + 1, R_RES + ZB, (d, mate))
 
     @pl.when(inner)
     def _():
-        clear_rows()
-        other_half(ZB, 2, 0, (d, mate))
-        other_half(ZB, 2, 1, (d, mate))
+        other_half(ZB, 2, 0, mate, (d, mate))
+        other_half(ZB, 2, 1, mate, (d, mate))
         row_b.start()
         clear_rows()
 
-    other_half(ZA, 1, 1, (d, from_a))
+    other_half(ZA, 1, 0, from_a, (d, from_a))
+    other_half(ZA, 1, 1, from_a, (d, from_a), last=True)
     row_a.start()
 
-    back = remote(rowres.at[3], rbuf.at[SLOTS + 2], 9, R_RES + SLOTS + 2, (d - 4, 3))
+    back = remote(rowres.at[3], rbuf.at[SLOTS + 2], S_ROW + 2, R_RES + SLOTS + 2, (d - 4, 3))
 
     @pl.when(corner_in)
     def _():
-        remote(buf.at[OWN, tail], corner, 3, R_CORNER, (d - 4, 3)).wait_recv()
+        remote(buf.at[OWN, tail], corner, S_CORNER, R_CORNER, (d - 4, 3)).wait_recv()
         first = buf[OWN, 0:16, :].astype(jnp.float32)[0:1]
         last = corner[0:16, :].astype(jnp.float32)[15:16]
         cos = jnp.sum(first * last, axis=1, keepdims=True)
@@ -308,23 +328,11 @@
         rowres[3, 1] = jnp.where(theirs, mass, 0.0)
         back.start()
 
-    def result(k):
-        return remote(
-            cacc.at[REACH + k],
-            rbuf.at[REACH - k],
-            S_RES + REACH + k,
-            R_RES + REACH - k,
-            (d + k, z),
-        )
-
-    for k in (-3, -2, -1, 1, 2, 3):
-        pl.when(has(k))(result(k).start)
-
     top_ref[...] = jnp.max(jnp.maximum(rowres[0, 0], cacc[OWN, 0]), axis=0, keepdims=True)
     mass_ref[...] = jnp.sum(rowres[0, 1] + cacc[OWN, 1], axis=0, keepdims=True)
 
     def add_result(slot):
-        remote(rowres.at[0], rbuf.at[slot], 7, R_RES + slot, (sister, z)).wait_recv()
+        remote(rowres.at[0], rbuf.at[slot], S_ROW, R_RES + slot, (sister, z)).wait_recv()
         top_ref[...] = jnp.maximum(
             top_ref[...], jnp.max(rbuf[slot, 0], axis=0, keepdims=True)
         )
@@ -339,13 +347,14 @@
     for part in range(3):
         z_copy(part, ZA, (d, to_a)).wait_send()
         pl.when(outer)(z_copy(part, ZB, (d, mate)).wait_send)
-    send_near.wait_send()
-    pl.when(has_far)(send_far.wait_send)
-    send_sis.wait_send()
+    for part in range(2):
+        send_near[part].wait_send()
+        pl.when(has_far)(send_far[part].wait_send)
+        send_sis[part].wait_send()
+        pl.when(has_across)(go_across[part].wait_send)
+        go_near[part].wait_send()
+        pl.when(has_diag)(go_diag[part].wait_send)
     pl.when(corner_out)(send_corner.wait_send)
-    pl.when(has_across)(go_across.wait_send)
-    go_near.wait_send()
-    pl.when(has_diag)(go_diag.wait_send)
     for k in (-3, -2, -1, 1, 2, 3):
         pl.when(has(k))(result(k).wait_send)
     row_a.wait_send()
@@ -375,7 +384,7 @@
             pltpu.SemaphoreType.DMA((2,)),
         ],
         compiler_params=pltpu.CompilerParams(
-            collective_id=0, has_side_effects=True, vmem_limit_bytes=32 * 2**20
+            collective_id=0, has_side_effects=True, vmem_limit_bytes=63 * 2**20
         ),
         name="dedup",
     )(embeds, cluster.reshape(1, q))

time: 43.6 us -> 41 us (0.940)
  the two profiles are of different devices: /device:TPU:5 before, /device:TPU:4 now
where the time goes in v3:
time: 41 us; the launch traced here: 40.8 us
  Pallas kernels  38.3 us (93%)
  local copies, waits for them, and re-layouts  1.86 us (5%)
  between operations  0.65 us (2%)
    pallas_call x1, Pallas kernels, per_device(): pl.pallas_call(functools.partial(kernel, n), out_shape=(jax.ShapeDtypeStr...  38.3 us
    unnamed x6, local copies, waits for them, and re-layouts  1.86 us

profile of v3, /device:TPU:4, one launch (start us, length us, event | category | flops | bytes accessed | tf_op | source)
XLA Modules:
  0.0 40.8 jit_solution(9715630736189497772)
XLA Ops:
  0.6 38.3 %dedup.1 = (f32[1,256]{1,0:T(1,128)}, f32[1,256]{1,0:T(1,128)}) custom-call(bf16[256,1024]{1,0:T(8,128)(2,1)} %e_hbm.1, s32[1,256]{1,0:T(1,128)} %bitcast.3), custom_call_target="tpu_custom_call" | custom-call | tf_op jit(solution)/shard_map/dedup/pallas_call | solution.py:367
  38.9 0.0 copy-start.1
  38.9 0.7 %copy-done.1 = f32[1,256]{1,0:T(1,128)S(1)} copy-done((f32[1,256]{1,0:T(1,128)S(1)}, f32[1,256]{1,0:T(1,128)}, u32[]{:S(2)}) %copy-start.1) | copy-done | bytes 1048
  39.6 0.0 copy-start
  39.6 0.6 %copy.6 = f32[256]{0:T(256)} copy(f32[256]{0:T(256)S(1)} %bitcast.5) | data formatting | bytes 2048
  40.2 0.1 copy-done
  40.2 0.6 %copy.7 = f32[256]{0:T(256)} copy(f32[256]{0:T(256)S(1)} %bitcast.4) | data formatting | bytes 2048
Async XLA Ops:
  38.9 0.7 %copy-start.1 = (f32[1,256]{1,0:T(1,128)S(1)}, f32[1,256]{1,0:T(1,128)}, u32[]{:S(2)}) copy-start(f32[1,256]{1,0:T(1,128)} %get-tuple-element.4) | copy-start | bytes 3076
  39.6 0.6 %copy-start = (f32[1,256]{1,0:T(1,128)S(1)}, f32[1,256]{1,0:T(1,128)}, u32[]{:S(2)}) copy-start(f32[1,256]{1,0:T(1,128)} %get-tuple-element.5) | copy-start | bytes 3076

commit v4 on v3

--- a/solution.py
+++ b/solution.py
@@ -28,8 +28,7 @@
     n,
     e_hbm,
     c_hbm,
-    top_ref,
-    mass_ref,
+    out_ref,
     e_ref,
     c_ref,
     buf,
@@ -159,14 +158,10 @@
     def take_ids(slot):
         return buf[slot, q : q + 16, 0:q].astype(jnp.float32)[0:1]
 
-    def load_x(slot):
-        xids[...] = jnp.broadcast_to(take_ids(slot), (128, q)).T
-
-    def clear_rows():
-        racc[0] = jnp.full((q, 128), -1.0, jnp.float32)
-        racc[1] = jnp.zeros((q, 128), jnp.float32)
-
-    def tile(xslot, start, size, slot, diagonal=False):
+    def load_x(slot, xi):
+        xids[xi] = jnp.broadcast_to(take_ids(slot), (128, q)).T
+
+    def tile(xslot, xi, start, size, slot, diagonal=False):
         rows = pl.ds(start, size)
         scores = lax.dot_general(
             buf[xslot, rows, :],
@@ -175,7 +170,7 @@
             preferred_element_type=jnp.float32,
         )
         yid = take_ids(slot)
-        xid = xids[rows, :]
+        xid = xids[xi, rows, :]
         tops, masses = [], []
         for lo in range(0, q, 128):
             mask = xid == yid[:, lo : lo + 128]
@@ -193,20 +188,23 @@
             tops.append(top)
             masses.append(mass)
         if not diagonal:
-            racc[0, rows, :] = jnp.maximum(racc[0, rows, :], functools.reduce(jnp.maximum, tops))
-            racc[1, rows, :] += functools.reduce(jnp.add, masses)
+            racc[xi, 0, rows, :] = jnp.maximum(
+                racc[xi, 0, rows, :], functools.reduce(jnp.maximum, tops)
+            )
+            racc[xi, 1, rows, :] += functools.reduce(jnp.add, masses)
 
     def row_result(xi, start, size):
         rows = pl.ds(start, size)
-        rowres[xi, 0, :, rows] = jnp.max(racc[0, rows, :].T.reshape(16, 8, size), axis=0)
-        rowres[xi, 1, :, rows] = jnp.sum(racc[1, rows, :].T.reshape(16, 8, size), axis=0)
+        rowres[xi, 0, :, rows] = jnp.max(racc[xi, 0, rows, :].T.reshape(16, 8, size), axis=0)
+        rowres[xi, 1, :, rows] = jnp.sum(racc[xi, 1, rows, :].T.reshape(16, 8, size), axis=0)
 
     cacc[:, 0] = jnp.full((SLOTS, 8, q), -1.0, jnp.float32)
     cacc[:, 1] = jnp.zeros((SLOTS, 8, q), jnp.float32)
 
-    load_x(OWN)
-    clear_rows()
-    tile(OWN, 0, q, OWN, diagonal=True)
+    racc[:, 0] = jnp.full((3, q, 128), -1.0, jnp.float32)
+    racc[:, 1] = jnp.zeros((3, q, 128), jnp.float32)
+    load_x(OWN, 0)
+    tile(OWN, 0, 0, q, OWN, diagonal=True)
 
     def arrived(slot, parts=(0, 1)):
         copies = halves(OWN, slot, 0, (sister, z))
@@ -246,23 +244,17 @@
 
         @pl.when((k > 0) & has(k))
         def _():
-            tile(OWN, 0, q, REACH + k)
+            tile(OWN, 0, 0, q, REACH + k)
 
         return carry
 
     lax.fori_loop(1, 4, own_step, 0)
 
-    @pl.when(has_diag)
-    def _():
-        for part in range(2):
+    def diag(part):
+        @pl.when(has_diag)
+        def _():
             arrived(REACH - near, (part,))
             go_diag[part].start()
-
-    pl.when(has(near + sis))(functools.partial(arrived, REACH + near + sis))
-    pl.when(has(-near + sis))(functools.partial(arrived, REACH - near + sis))
-    lax.fori_loop(4, SLOTS, own_step, 0)
-    row_result(0, 0, q)
-    clear_rows()
 
     def result(k):
         return remote(
@@ -273,39 +265,56 @@
             (d + k, z),
         )
 
-    def other_half(slot, xi, part, xz, dev, last=False):
-        if part == 0:
-            z_copy(2, slot, dev).wait_recv()
-        load_x(slot)
-        z_copy(part, slot, dev).wait_recv()
-
+    def meet(slot, xi, xz, start, size, first, stop, last=False):
         def step(i, carry):
-            k = i - REACH
+            k = nth(i)
             apart = ((k == REACH) & (xz < z - 1)) | ((k == -REACH) & (z < xz - 1))
 
             @pl.when(has(k) & jnp.logical_not(apart))
             def _():
-                tile(slot, part * half, half, i)
+                tile(slot, xi, start, size, REACH + k)
 
             if last:
                 pl.when(has(k) & (k != 0))(lambda: result(k).start())
             return carry
 
-        lax.fori_loop(0, SLOTS, step, 0)
-        row_result(xi, part * half, half)
+        lax.fori_loop(first, stop, step, 0)
 
     row_a = remote(rowres.at[1], rbuf.at[ZA], S_ROW, R_RES + ZA, (d, from_a))
     row_b = remote(rowres.at[2], rbuf.at[ZB], S_ROW + 1, R_RES + ZB, (d, mate))
 
+    diag(0)
+
     @pl.when(inner)
     def _():
-        other_half(ZB, 2, 0, mate, (d, mate))
-        other_half(ZB, 2, 1, mate, (d, mate))
+        z_copy(2, ZB, (d, mate)).wait_recv()
+        load_x(ZB, 2)
+        for part in range(2):
+            z_copy(part, ZB, (d, mate)).wait_recv()
+        meet(ZB, 2, mate, 0, q, 0, 4)
+
+    diag(1)
+    z_copy(2, ZA, (d, from_a)).wait_recv()
+    load_x(ZA, 1)
+    z_copy(0, ZA, (d, from_a)).wait_recv()
+    meet(ZA, 1, from_a, 0, half, 0, 4)
+
+    pl.when(has(near + sis))(functools.partial(arrived, REACH + near + sis))
+    pl.when(has(-near + sis))(functools.partial(arrived, REACH - near + sis))
+    lax.fori_loop(4, SLOTS, own_step, 0)
+    row_result(0, 0, q)
+
+    @pl.when(inner)
+    def _():
+        meet(ZB, 2, mate, 0, q, 4, SLOTS)
+        row_result(2, 0, q)
         row_b.start()
-        clear_rows()
-
-    other_half(ZA, 1, 0, from_a, (d, from_a))
-    other_half(ZA, 1, 1, from_a, (d, from_a), last=True)
+
+    meet(ZA, 1, from_a, 0, half, 4, SLOTS)
+    row_result(1, 0, half)
+    z_copy(1, ZA, (d, from_a)).wait_recv()
+    meet(ZA, 1, from_a, half, half, 0, SLOTS, last=True)
+    row_result(1, half, half)
     row_a.start()
 
     back = remote(rowres.at[3], rbuf.at[SLOTS + 2], S_ROW + 2, R_RES + SLOTS + 2, (d - 4, 3))
@@ -328,15 +337,13 @@
         rowres[3, 1] = jnp.where(theirs, mass, 0.0)
         back.start()
 
-    top_ref[...] = jnp.max(jnp.maximum(rowres[0, 0], cacc[OWN, 0]), axis=0, keepdims=True)
-    mass_ref[...] = jnp.sum(rowres[0, 1] + cacc[OWN, 1], axis=0, keepdims=True)
+    out_ref[0] = jnp.maximum(rowres[0, 0], cacc[OWN, 0])
+    out_ref[1] = rowres[0, 1] + cacc[OWN, 1]
 
     def add_result(slot):
         remote(rowres.at[0], rbuf.at[slot], S_ROW, R_RES + slot, (sister, z)).wait_recv()
-        top_ref[...] = jnp.maximum(
-            top_ref[...], jnp.max(rbuf[slot, 0], axis=0, keepdims=True)
-        )
-        mass_ref[...] += jnp.sum(rbuf[slot, 1], axis=0, keepdims=True)
+        out_ref[0] = jnp.maximum(out_ref[0], rbuf[slot, 0])
+        out_ref[1] += rbuf[slot, 1]
 
     pl.when(corner_out)(functools.partial(add_result, SLOTS + 2))
     for k in (-3, -2, -1, 1, 2, 3):
@@ -362,20 +369,25 @@
     pl.when(corner_in)(back.wait_send)
 
 
+def finish(both_ref, top_ref, mass_ref):
+    top_ref[...] = jnp.max(both_ref[0], axis=0)
+    mass_ref[...] = jnp.sum(both_ref[1], axis=0)
+
+
 def per_device(n, embeds, cluster):
     q, width = embeds.shape
-    top, mass = pl.pallas_call(
+    both = pl.pallas_call(
         functools.partial(kernel, n),
-        out_shape=(jax.ShapeDtypeStruct((1, q), jnp.float32),) * 2,
+        out_shape=jax.ShapeDtypeStruct((2, 8, q), jnp.float32),
         in_specs=[pl.BlockSpec(memory_space=pltpu.HBM)] * 2,
-        out_specs=(pl.BlockSpec(memory_space=pltpu.VMEM),) * 2,
+        out_specs=pl.BlockSpec(memory_space=pltpu.VMEM),
         scratch_shapes=[
             pltpu.VMEM((q, width), jnp.bfloat16),
             pltpu.VMEM((1, q), jnp.int32),
             pltpu.VMEM((SLOTS + 2, q + 16, width), jnp.bfloat16),
             pltpu.VMEM((32, width), jnp.bfloat16),
-            pltpu.VMEM((q, 128), jnp.float32),
-            pltpu.VMEM((2, q, 128), jnp.float32),
+            pltpu.VMEM((3, q, 128), jnp.float32),
+            pltpu.VMEM((3, 2, q, 128), jnp.float32),
             pltpu.VMEM((SLOTS, 2, 8, q), jnp.float32),
             pltpu.VMEM((4, 2, 8, q), jnp.float32),
             pltpu.VMEM((SLOTS + 3, 2, 8, q), jnp.float32),
@@ -388,7 +400,13 @@
         ),
         name="dedup",
     )(embeds, cluster.reshape(1, q))
-    return top.reshape(q), mass.reshape(q)
+    return pl.pallas_call(
+        finish,
+        out_shape=(jax.ShapeDtypeStruct((q,), jnp.float32),) * 2,
+        in_specs=[pl.BlockSpec(memory_space=pltpu.VMEM)],
+        out_specs=(pl.BlockSpec(memory_space=pltpu.VMEM),) * 2,
+        name="finish",
+    )(both)
 
 
 def solution(mesh):

time: 41 us -> 38.6 us (0.941)
  the two profiles are of different devices: /device:TPU:4 before, /device:TPU:0 now
where the time goes in v4:
time: 38.6 us; the launch traced here: 38.3 us
  Pallas kernels  37.7 us (98%)
  between operations  0.64 us (2%)
    pallas_call x1, Pallas kernels, per_device(): pl.pallas_call(functools.partial(kernel, n), out_shape=jax.ShapeDtypeStru...  36.4 us
    pallas_call x1, Pallas kernels, per_device(): pl.pallas_call(finish, out_shape=(jax.ShapeDtypeStruct((q,), jnp.float32)...  1.3 us

profile of v4, /device:TPU:0, one launch (start us, length us, event | category | flops | bytes accessed | tf_op | source)
XLA Modules:
  0.0 38.3 jit_solution(222525073888643114)
XLA Ops:
  0.6 36.4 %dedup.1.both_ref = f32[2,8,256]{2,1,0:T(8,128)} custom-call(bf16[256,1024]{1,0:T(8,128)(2,1)} %e_hbm.1, s32[1,256]{1,0:T(1,128)} %bitcast.1), custom_call_target="tpu_custom_call" | custom-call | tf_op jit(solution)/shard_map/dedup/pallas_call | solution.py:379
  37.0 1.3 %finish.1 = (f32[256]{0:T(256)}, f32[256]{0:T(256)}) custom-call(f32[2,8,256]{2,1,0:T(8,128)} %dedup.1.both_ref), custom_call_target="tpu_custom_call" | custom-call | tf_op jit(solution)/shard_map/finish/pallas_call | solution.py:403

commit v5 on v4

--- a/solution.py
+++ b/solution.py
@@ -44,6 +44,7 @@
 ):
     q, width = e_ref.shape
     half = q // 2
+    most = 3 * q // 4
     d = lax.axis_index("docs")
     z = lax.axis_index("rep")
     odd = lax.rem(d, 2)
@@ -106,7 +107,7 @@
         if part == 2:
             view = (id_rows, pl.ds(0, q))
         else:
-            view = (pl.ds(part * half, half),)
+            view = (pl.ds(0, most) if part == 0 else pl.ds(most, q - most),)
         return remote(
             buf.at[(OWN,) + view],
             buf.at[(slot,) + view],
@@ -137,19 +138,17 @@
     buf[OWN, q : q + 16, :] = jnp.zeros((16, width), jnp.bfloat16)
     buf[OWN, q : q + 16, 0:q] = jnp.broadcast_to(ids, (16, q)).astype(jnp.bfloat16)
     load_e.wait()
-    for part in range(2):
-        rows = pl.ds(part * half, half)
+    for part, rows in enumerate((pl.ds(0, most), pl.ds(most, q - most))):
         x = e_ref[rows, :].astype(jnp.float32)
         scale = lax.rsqrt(jnp.mean(x * x, axis=1, keepdims=True) + 1e-06)
         buf[OWN, rows, :] = (x * scale * width ** (-0.5)).astype(jnp.bfloat16)
         if part == 0:
             pl.semaphore_wait(barrier, total)
+            send_z(2)
+        send_z(part)
+        send_near[part].start()
         pl.when(has_far)(send_far[part].start)
-        send_near[part].start()
-        send_z(part)
         send_sis[part].start()
-        if part == 0:
-            send_z(2)
     pl.when(corner_out)(send_corner.start)
 
     lanes = lax.broadcasted_iota(jnp.int32, (8, q), 1)
@@ -297,7 +296,7 @@
     z_copy(2, ZA, (d, from_a)).wait_recv()
     load_x(ZA, 1)
     z_copy(0, ZA, (d, from_a)).wait_recv()
-    meet(ZA, 1, from_a, 0, half, 0, 4)
+    meet(ZA, 1, from_a, 0, most, 0, 4)
 
     pl.when(has(near + sis))(functools.partial(arrived, REACH + near + sis))
     pl.when(has(-near + sis))(functools.partial(arrived, REACH - near + sis))
@@ -310,11 +309,10 @@
         row_result(2, 0, q)
         row_b.start()
 
-    meet(ZA, 1, from_a, 0, half, 4, SLOTS)
-    row_result(1, 0, half)
+    meet(ZA, 1, from_a, 0, most, 4, SLOTS)
     z_copy(1, ZA, (d, from_a)).wait_recv()
-    meet(ZA, 1, from_a, half, half, 0, SLOTS, last=True)
-    row_result(1, half, half)
+    meet(ZA, 1, from_a, most, q - most, 0, SLOTS, last=True)
+    row_result(1, 0, q)
     row_a.start()
 
     back = remote(rowres.at[3], rbuf.at[SLOTS + 2], S_ROW + 2, R_RES + SLOTS + 2, (d - 4, 3))
@@ -400,13 +398,7 @@
         ),
         name="dedup",
     )(embeds, cluster.reshape(1, q))
-    return pl.pallas_call(
-        finish,
-        out_shape=(jax.ShapeDtypeStruct((q,), jnp.float32),) * 2,
-        in_specs=[pl.BlockSpec(memory_space=pltpu.VMEM)],
-        out_specs=(pl.BlockSpec(memory_space=pltpu.VMEM),) * 2,
-        name="finish",
-    )(both)
+    return jnp.max(both[0], axis=0), jnp.sum(both[1], axis=0)
 
 
 def solution(mesh):

time: 38.6 us -> 40.6 us (1.052)
  the two profiles are of different devices: /device:TPU:0 before, /device:TPU:11 now
where the time goes in v5:
time: 40.6 us; the launch traced here: 40.4 us
  Pallas kernels  38.5 us (95%)
  other arithmetic  1.29 us (3%)
  between operations  0.64 us (2%)
    pallas_call x1, Pallas kernels, per_device(): pl.pallas_call(functools.partial(kernel, n), out_shape=jax.ShapeDtypeStru...  38.5 us
    reduce_sum x1, other arithmetic, per_device(): return (jnp.max(both[0], axis=0), jnp.sum(both[1], axis=0))  1.29 us

profile of v5, /device:TPU:11, one launch (start us, length us, event | category | flops | bytes accessed | tf_op | source)
XLA Modules:
  0.0 40.4 jit_solution(5863364863209194002)
XLA Ops:
  0.6 38.5 %dedup.1 = f32[2,8,256]{2,1,0:T(8,128)} custom-call(bf16[256,1024]{1,0:T(8,128)(2,1)} %e_hbm.1, s32[1,256]{1,0:T(1,128)} %bitcast.1), custom_call_target="tpu_custom_call" | custom-call | tf_op jit(solution)/shard_map/dedup/pallas_call | solution.py:377
  39.1 1.3 %slice_reduce_fusion = (f32[256]{0:T(256)}, f32[256]{0:T(256)}) fusion(f32[2,8,256]{2,1,0:T(8,128)} %dedup.1), kind=kLoop, calls=%fused_computation | loop fusion | flops 3584 | bytes 18432 | tf_op jit(solution)/shard_map/reduce_sum | solution.py:401

commit v6 on v4

--- a/solution.py
+++ b/solution.py
@@ -15,11 +15,12 @@
 REACH = 3
 SLOTS = 2 * REACH + 1
 OWN, ZA, ZB = REACH, SLOTS, SLOTS + 1
-S_CORNER = 12
+PARTS = 4
+S_CORNER = 6 * PARTS
 S_ROW = S_CORNER + 1
 S_RES = S_ROW + 3
 S_Z = S_RES + SLOTS
-R_CORNER = 2 * SLOTS
+R_CORNER = PARTS * SLOTS
 R_RES = R_CORNER + 1
 R_Z = R_RES + SLOTS + 3
 
@@ -119,15 +120,18 @@
         pl.when(outer)(z_copy(part, ZB, (d, mate)).start)
         z_copy(part, ZA, (d, to_a)).start()
 
-    def halves(slot, to, s, dev):
+    def pieces(slot, to, s, dev):
+        size = q // PARTS
+        views = [pl.ds(part * size, size) for part in range(PARTS - 1)]
+        views.append(pl.ds(q - size, size + 16))
         return [
-            remote(buf.at[slot, view], buf.at[to, view], 2 * s + part, 2 * to + part, dev)
-            for part, view in enumerate((pl.ds(0, half), pl.ds(half, half + 16)))
+            remote(buf.at[slot, view], buf.at[to, view], PARTS * s + part, PARTS * to + part, dev)
+            for part, view in enumerate(views)
         ]
 
-    send_near = halves(OWN, REACH - near, 0, (d + near, z))
-    send_far = halves(OWN, REACH - far, 1, (d + far, z))
-    send_sis = halves(OWN, REACH - sis, 2, (sister, z))
+    send_near = pieces(OWN, REACH - near, 0, (d + near, z))
+    send_far = pieces(OWN, REACH - far, 1, (d + far, z))
+    send_sis = pieces(OWN, REACH - sis, 2, (sister, z))
     has_far = has(far)
     tail = pl.ds(q - 16, 32)
     send_corner = remote(buf.at[OWN, tail], corner, S_CORNER, R_CORNER, (d + 4, 0))
@@ -144,10 +148,13 @@
         buf[OWN, rows, :] = (x * scale * width ** (-0.5)).astype(jnp.bfloat16)
         if part == 0:
             pl.semaphore_wait(barrier, total)
-        pl.when(has_far)(send_far[part].start)
-        send_near[part].start()
+        ready = range(part * PARTS // 2, (part + 1) * PARTS // 2)
+        for piece in ready:
+            pl.when(has_far)(send_far[piece].start)
+            send_near[piece].start()
         send_z(part)
-        send_sis[part].start()
+        for piece in ready:
+            send_sis[piece].start()
         if part == 0:
             send_z(2)
     pl.when(corner_out)(send_corner.start)
@@ -206,8 +213,8 @@
     load_x(OWN, 0)
     tile(OWN, 0, 0, q, OWN, diagonal=True)
 
-    def arrived(slot, parts=(0, 1)):
-        copies = halves(OWN, slot, 0, (sister, z))
+    def arrived(slot, parts=range(PARTS)):
+        copies = pieces(OWN, slot, 0, (sister, z))
         for part in parts:
             copies[part].wait_recv()
 
@@ -216,14 +223,14 @@
     has_across = has(across) & has(across_from)
 
     def go_on(slot, s, by):
-        return halves(slot, slot - by, s, (d + by, z))
+        return pieces(slot, slot - by, s, (d + by, z))
 
     go_across = go_on(REACH + across_from, 3, across)
     go_near = go_on(REACH + near, 4, sis)
     go_diag = go_on(REACH - near, 5, sis)
     has_diag = has(-near)
 
-    for part in range(2):
+    for part in range(PARTS):
         pl.when(has_far)(functools.partial(arrived, REACH + far, (part,)))
         pl.when(has_across & jnp.logical_not(ends))(go_across[part].start)
         arrived(REACH + near, (part,))
@@ -283,7 +290,8 @@
     row_a = remote(rowres.at[1], rbuf.at[ZA], S_ROW, R_RES + ZA, (d, from_a))
     row_b = remote(rowres.at[2], rbuf.at[ZB], S_ROW + 1, R_RES + ZB, (d, mate))
 
-    diag(0)
+    for part in range(PARTS // 2):
+        diag(part)
 
     @pl.when(inner)
     def _():
@@ -293,12 +301,8 @@
             z_copy(part, ZB, (d, mate)).wait_recv()
         meet(ZB, 2, mate, 0, q, 0, 4)
 
-    diag(1)
-    z_copy(2, ZA, (d, from_a)).wait_recv()
-    load_x(ZA, 1)
-    z_copy(0, ZA, (d, from_a)).wait_recv()
-    meet(ZA, 1, from_a, 0, half, 0, 4)
-
+    for part in range(PARTS // 2, PARTS):
+        diag(part)
     pl.when(has(near + sis))(functools.partial(arrived, REACH + near + sis))
     pl.when(has(-near + sis))(functools.partial(arrived, REACH - near + sis))
     lax.fori_loop(4, SLOTS, own_step, 0)
@@ -310,7 +314,10 @@
         row_result(2, 0, q)
         row_b.start()
 
-    meet(ZA, 1, from_a, 0, half, 4, SLOTS)
+    z_copy(2, ZA, (d, from_a)).wait_recv()
+    load_x(ZA, 1)
+    z_copy(0, ZA, (d, from_a)).wait_recv()
+    meet(ZA, 1, from_a, 0, half, 0, SLOTS)
     row_result(1, 0, half)
     z_copy(1, ZA, (d, from_a)).wait_recv()
     meet(ZA, 1, from_a, half, half, 0, SLOTS, last=True)
@@ -354,7 +361,7 @@
     for part in range(3):
         z_copy(part, ZA, (d, to_a)).wait_send()
         pl.when(outer)(z_copy(part, ZB, (d, mate)).wait_send)
-    for part in range(2):
+    for part in range(PARTS):
         send_near[part].wait_send()
         pl.when(has_far)(send_far[part].wait_send)
         send_sis[part].wait_send()

time: 38.6 us -> 39 us (1.010)
  no operation moved by 1% of the time
where the time goes in v6:
time: 39 us; the launch traced here: 38.6 us
  Pallas kernels  37.9 us (97%)
  between operations  0.64 us (2%)
    pallas_call x1, Pallas kernels, per_device(): pl.pallas_call(functools.partial(kernel, n), out_shape=jax.ShapeDtypeStru...  36.6 us
    pallas_call x1, Pallas kernels, per_device(): pl.pallas_call(finish, out_shape=(jax.ShapeDtypeStruct((q,), jnp.float32)...  1.3 us

profile of v6, /device:TPU:0, one launch (start us, length us, event | category | flops | bytes accessed | tf_op | source)
XLA Modules:
  0.0 38.6 jit_solution(5660548036067541212)
XLA Ops:
  0.6 36.6 %dedup.1.both_ref = f32[2,8,256]{2,1,0:T(8,128)} custom-call(bf16[256,1024]{1,0:T(8,128)(2,1)} %e_hbm.1, s32[1,256]{1,0:T(1,128)} %bitcast.1), custom_call_target="tpu_custom_call" | custom-call | tf_op jit(solution)/shard_map/dedup/pallas_call | solution.py:386
  37.3 1.3 %finish.1 = (f32[256]{0:T(256)}, f32[256]{0:T(256)}) custom-call(f32[2,8,256]{2,1,0:T(8,128)} %dedup.1.both_ref), custom_call_target="tpu_custom_call" | custom-call | tf_op jit(solution)/shard_map/finish/pallas_call | solution.py:410

commit v7 on v4

--- a/solution.py
+++ b/solution.py
@@ -81,10 +81,16 @@
     def greet(dev):
         pl.semaphore_signal(barrier, inc=1, device_id=dev, device_id_type=MESH)
 
-    load_e = pltpu.make_async_copy(e_hbm, e_ref, lsem.at[0])
-    load_c = pltpu.make_async_copy(c_hbm, c_ref, lsem.at[1])
-    load_e.start()
+    bands = [pl.ds(i * q // 4, q // 4) for i in range(4)]
+    load_e = [
+        pltpu.make_async_copy(e_hbm.at[rows], e_ref.at[rows], lsem.at[i])
+        for i, rows in enumerate(bands)
+    ]
+    load_c = pltpu.make_async_copy(c_hbm, c_ref, lsem.at[4])
+    load_e[0].start()
     load_c.start()
+    for load in load_e[1:]:
+        load.start()
     total = jnp.int32(3)
     for k in (-3, -2, -1, 1, 2, 3):
         pl.when(has(k))(functools.partial(greet, (d + k, z)))
@@ -132,16 +138,12 @@
     tail = pl.ds(q - 16, 32)
     send_corner = remote(buf.at[OWN, tail], corner, S_CORNER, R_CORNER, (d + 4, 0))
 
-    load_c.wait()
-    ids = c_ref[...].astype(jnp.float32)
-    buf[OWN, q : q + 16, :] = jnp.zeros((16, width), jnp.bfloat16)
-    buf[OWN, q : q + 16, 0:q] = jnp.broadcast_to(ids, (16, q)).astype(jnp.bfloat16)
-    load_e.wait()
     for part in range(2):
-        rows = pl.ds(part * half, half)
-        x = e_ref[rows, :].astype(jnp.float32)
-        scale = lax.rsqrt(jnp.mean(x * x, axis=1, keepdims=True) + 1e-06)
-        buf[OWN, rows, :] = (x * scale * width ** (-0.5)).astype(jnp.bfloat16)
+        for i in (2 * part, 2 * part + 1):
+            load_e[i].wait()
+            x = e_ref[bands[i], :].astype(jnp.float32)
+            scale = lax.rsqrt(jnp.mean(x * x, axis=1, keepdims=True) + 1e-06)
+            buf[OWN, bands[i], :] = (x * scale * width ** (-0.5)).astype(jnp.bfloat16)
         if part == 0:
             pl.semaphore_wait(barrier, total)
         pl.when(has_far)(send_far[part].start)
@@ -149,6 +151,10 @@
         send_z(part)
         send_sis[part].start()
         if part == 0:
+            load_c.wait()
+            ids = c_ref[...].astype(jnp.float32)
+            buf[OWN, q : q + 16, :] = jnp.zeros((16, width), jnp.bfloat16)
+            buf[OWN, q : q + 16, 0:q] = jnp.broadcast_to(ids, (16, q)).astype(jnp.bfloat16)
             send_z(2)
     pl.when(corner_out)(send_corner.start)
 
@@ -393,7 +399,7 @@
             pltpu.VMEM((SLOTS + 3, 2, 8, q), jnp.float32),
             pltpu.SemaphoreType.DMA((S_Z + 6,)),
             pltpu.SemaphoreType.DMA((R_Z + 6,)),
-            pltpu.SemaphoreType.DMA((2,)),
+            pltpu.SemaphoreType.DMA((5,)),
         ],
         compiler_params=pltpu.CompilerParams(
             collective_id=0, has_side_effects=True, vmem_limit_bytes=63 * 2**20

time: 38.6 us -> 38.6 us (level)
  no operation moved by 1% of the time
where the time goes in v7:
time: 38.6 us; the launch traced here: 38.4 us
  Pallas kernels  37.7 us (98%)
  between operations  0.64 us (2%)
    pallas_call x1, Pallas kernels, per_device(): pl.pallas_call(functools.partial(kernel, n), out_shape=jax.ShapeDtypeStru...  36.4 us
    pallas_call x1, Pallas kernels, per_device(): pl.pallas_call(finish, out_shape=(jax.ShapeDtypeStruct((q,), jnp.float32)...  1.3 us

profile of v7, /device:TPU:0, one launch (start us, length us, event | category | flops | bytes accessed | tf_op | source)
XLA Modules:
  0.0 38.4 jit_solution(7688574436873365520)
XLA Ops:
  0.6 36.4 %dedup.1.both_ref = f32[2,8,256]{2,1,0:T(8,128)} custom-call(bf16[256,1024]{1,0:T(8,128)(2,1)} %e_hbm.1, s32[1,256]{1,0:T(1,128)} %bitcast.1), custom_call_target="tpu_custom_call" | custom-call | tf_op jit(solution)/shard_map/dedup/pallas_call | solution.py:385
  37.1 1.3 %finish.1 = (f32[256]{0:T(256)}, f32[256]{0:T(256)}) custom-call(f32[2,8,256]{2,1,0:T(8,128)} %dedup.1.both_ref), custom_call_target="tpu_custom_call" | custom-call | tf_op jit(solution)/shard_map/finish/pallas_call | solution.py:409

commit v8 on v4

--- a/solution.py
+++ b/solution.py
@@ -396,7 +396,7 @@
             pltpu.SemaphoreType.DMA((2,)),
         ],
         compiler_params=pltpu.CompilerParams(
-            collective_id=0, has_side_effects=True, vmem_limit_bytes=63 * 2**20
+            collective_id=0, has_side_effects=True, vmem_limit_bytes=215 * 2**18
         ),
         name="dedup",
     )(embeds, cluster.reshape(1, q))

time: 38.6 us -> 39.2 us (1.016)
  local copies, waits for them, and re-layouts: 0 us -> 1.26 us
  Pallas kernels: 37.7 us -> 37 us
    unnamed x0 -> x4, local copies, waits for them, and re-layouts: none -> 1.26 us
    pallas_call x1, Pallas kernels: 36.4 us -> 35.7 us  [per_device(): pl.pallas_call(functools.partial(kernel, n), out_shape=jax.ShapeDtypeStru...]
where the time goes in v8:
time: 39.2 us; the launch traced here: 39 us
  Pallas kernels  37 us (94%)
  local copies, waits for them, and re-layouts  1.26 us (3%)
  between operations  0.65 us (2%)
    pallas_call x1, Pallas kernels, per_device(): pl.pallas_call(functools.partial(kernel, n), out_shape=jax.ShapeDtypeStru...  35.7 us
    pallas_call x1, Pallas kernels, per_device(): pl.pallas_call(finish, out_shape=(jax.ShapeDtypeStruct((q,), jnp.float32)...  1.29 us
    unnamed x4, local copies, waits for them, and re-layouts  1.26 us

profile of v8, /device:TPU:0, one launch (start us, length us, event | category | flops | bytes accessed | tf_op | source)
XLA Modules:
  0.0 39.0 jit_solution(1143378353501721668)
XLA Ops:
  0.6 0.0 copy-start.1
  0.6 0.7 %copy-done.1 = s32[256]{0:T(256)S(1)} copy-done((s32[256]{0:T(256)S(1)}, s32[256]{0:T(256)}, u32[]{:S(2)}) %copy-start.1) | copy-done | bytes 1048
  1.3 35.7 %dedup.1.both_ref = f32[2,8,256]{2,1,0:T(8,128)S(1)} custom-call(bf16[256,1024]{1,0:T(8,128)(2,1)} %e_hbm.1, s32[1,256]{1,0:T(1,128)S(1)} %bitcast.1), custom_call_target="tpu_custom_call" | custom-call | tf_op jit(solution)/shard_map/dedup/pallas_call | solution.py:379
  37.1 0.0 copy-start
  37.1 0.6 %copy-done = f32[2,8,256]{2,1,0:T(8,128)} copy-done((f32[2,8,256]{2,1,0:T(8,128)}, f32[2,8,256]{2,1,0:T(8,128)S(1)}, u32[]{:S(2)}) %copy-start) | copy-done | bytes 16408
  37.7 1.3 %finish.1 = (f32[256]{0:T(256)}, f32[256]{0:T(256)}) custom-call(f32[2,8,256]{2,1,0:T(8,128)} %copy-done), custom_call_target="tpu_custom_call" | custom-call | tf_op jit(solution)/shard_map/finish/pallas_call | solution.py:403
Async XLA Ops:
  0.6 0.7 %copy-start.1 = (s32[256]{0:T(256)S(1)}, s32[256]{0:T(256)}, u32[]{:S(2)}) copy-start(s32[256]{0:T(256)} %param.3) | copy-start | bytes 3076
  37.1 0.6 %copy-start = (f32[2,8,256]{2,1,0:T(8,128)}, f32[2,8,256]{2,1,0:T(8,128)S(1)}, u32[]{:S(2)}) copy-start(f32[2,8,256]{2,1,0:T(8,128)S(1)} %dedup.1.both_ref) | copy-start | bytes 49156

commit v9 on v4

--- a/solution.py
+++ b/solution.py
@@ -56,8 +56,8 @@
     to_a = jnp.where(z < 2, z + 2, 3 - z)
     from_a = jnp.where(z < 2, 3 - z, z - 2)
     mate = z + 1 - 2 * lax.rem(z, 2)
-    inner = (z == 1) | (z == 2)
-    outer = (z == 0) | (z == 3)
+    takes_b = (z == 0) | (z == 3)
+    sends_b = (z == 1) | (z == 2)
 
     def has(k):
         return (d + k >= 0) & (d + k < n)
@@ -116,7 +116,7 @@
         )
 
     def send_z(part):
-        pl.when(outer)(z_copy(part, ZB, (d, mate)).start)
+        pl.when(sends_b)(z_copy(part, ZB, (d, mate)).start)
         z_copy(part, ZA, (d, to_a)).start()
 
     def halves(slot, to, s, dev):
@@ -285,7 +285,7 @@
 
     diag(0)
 
-    @pl.when(inner)
+    @pl.when(takes_b)
     def _():
         z_copy(2, ZB, (d, mate)).wait_recv()
         load_x(ZB, 2)
@@ -304,7 +304,7 @@
     lax.fori_loop(4, SLOTS, own_step, 0)
     row_result(0, 0, q)
 
-    @pl.when(inner)
+    @pl.when(takes_b)
     def _():
         meet(ZB, 2, mate, 0, q, 4, SLOTS)
         row_result(2, 0, q)
@@ -349,11 +349,11 @@
     for k in (-3, -2, -1, 1, 2, 3):
         pl.when(has(k))(functools.partial(add_result, REACH + k))
     add_result(ZA)
-    pl.when(outer)(functools.partial(add_result, ZB))
+    pl.when(sends_b)(functools.partial(add_result, ZB))
 
     for part in range(3):
         z_copy(part, ZA, (d, to_a)).wait_send()
-        pl.when(outer)(z_copy(part, ZB, (d, mate)).wait_send)
+        pl.when(sends_b)(z_copy(part, ZB, (d, mate)).wait_send)
     for part in range(2):
         send_near[part].wait_send()
         pl.when(has_far)(send_far[part].wait_send)
@@ -365,7 +365,7 @@
     for k in (-3, -2, -1, 1, 2, 3):
         pl.when(has(k))(result(k).wait_send)
     row_a.wait_send()
-    pl.when(inner)(row_b.wait_send)
+    pl.when(takes_b)(row_b.wait_send)
     pl.when(corner_in)(back.wait_send)
 
 

time: 38.6 us -> 43.7 us (1.13)
  Pallas kernels: 37.7 us -> 42.8 us
    pallas_call x1, Pallas kernels: 36.4 us -> 41.5 us  [per_device(): pl.pallas_call(functools.partial(kernel, n), out_shape=jax.ShapeDtypeStru...]
where the time goes in v9:
time: 43.7 us; the launch traced here: 43.4 us
  Pallas kernels  42.8 us (98%)
  between operations  0.64 us (1%)
    pallas_call x1, Pallas kernels, per_device(): pl.pallas_call(functools.partial(kernel, n), out_shape=jax.ShapeDtypeStru...  41.5 us
    pallas_call x1, Pallas kernels, per_device(): pl.pallas_call(finish, out_shape=(jax.ShapeDtypeStruct((q,), jnp.float32)...  1.3 us

profile of v9, /device:TPU:0, one launch (start us, length us, event | category | flops | bytes accessed | tf_op | source)
XLA Modules:
  0.0 43.4 jit_solution(17539556251096716323)
XLA Ops:
  0.6 41.5 %dedup.1.both_ref = f32[2,8,256]{2,1,0:T(8,128)} custom-call(bf16[256,1024]{1,0:T(8,128)(2,1)} %e_hbm.1, s32[1,256]{1,0:T(1,128)} %bitcast.1), custom_call_target="tpu_custom_call" | custom-call | tf_op jit(solution)/shard_map/dedup/pallas_call | solution.py:379
  42.1 1.3 %finish.1 = (f32[256]{0:T(256)}, f32[256]{0:T(256)}) custom-call(f32[2,8,256]{2,1,0:T(8,128)} %dedup.1.both_ref), custom_call_target="tpu_custom_call" | custom-call | tf_op jit(solution)/shard_map/finish/pallas_call | solution.py:403

commit v10 on v4

--- a/solution.py
+++ b/solution.py
@@ -144,8 +144,8 @@
         buf[OWN, rows, :] = (x * scale * width ** (-0.5)).astype(jnp.bfloat16)
         if part == 0:
             pl.semaphore_wait(barrier, total)
+        send_near[part].start()
         pl.when(has_far)(send_far[part].start)
-        send_near[part].start()
         send_z(part)
         send_sis[part].start()
         if part == 0:

time: 38.6 us -> 38.6 us (level)
  no operation moved by 1% of the time
where the time goes in v10:
time: 38.6 us; the launch traced here: 38.3 us
  Pallas kernels  37.7 us (98%)
  between operations  0.64 us (2%)
    pallas_call x1, Pallas kernels, per_device(): pl.pallas_call(functools.partial(kernel, n), out_shape=jax.ShapeDtypeStru...  36.4 us
    pallas_call x1, Pallas kernels, per_device(): pl.pallas_call(finish, out_shape=(jax.ShapeDtypeStruct((q,), jnp.float32)...  1.3 us

profile of v10, /device:TPU:0, one launch (start us, length us, event | category | flops | bytes accessed | tf_op | source)
XLA Modules:
  0.0 38.3 jit_solution(1174142298649223544)
XLA Ops:
  0.6 36.4 %dedup.1.both_ref = f32[2,8,256]{2,1,0:T(8,128)} custom-call(bf16[256,1024]{1,0:T(8,128)(2,1)} %e_hbm.1, s32[1,256]{1,0:T(1,128)} %bitcast.1), custom_call_target="tpu_custom_call" | custom-call | tf_op jit(solution)/shard_map/dedup/pallas_call | solution.py:379
  37.0 1.3 %finish.1 = (f32[256]{0:T(256)}, f32[256]{0:T(256)}) custom-call(f32[2,8,256]{2,1,0:T(8,128)} %dedup.1.both_ref), custom_call_target="tpu_custom_call" | custom-call | tf_op jit(solution)/shard_map/finish/pallas_call | solution.py:403
